TPU v7x, 32 devices: a whole 2x2x4 slice. The times are simulated.
32 devices in a mesh: dp: 16 (over z, y, x), seq: 2 (over core).
Axes of the slice: x: 2, y: 2, z: 4, core: 2. Of those that a mesh axis runs over, the one named last changes fastest.
Arguments:
- acts: bfloat16 [4096, 4096], P('dp', 'seq'), may hold values from -6 to 6
- upstream: bfloat16 [4096, 1024], P(('dp', 'seq')), may hold values from -0.0234375 to 0.0234375
- keep_lists: int32 [64, 8], replicated, may hold values from 0 to 15, all different within a row
- left_gram: float32 [2, 16, 16, 64, 64], P('seq', 'dp'), as said below
- right_gram: float32 [2, 16, 16, 64, 64], P('seq', 'dp'), as said below
- left_basis: float32 [2, 16, 16, 64, 64], P('seq', 'dp'), may hold values from -0.75 to 0.75
- right_basis: float32 [2, 16, 16, 64, 64], P('seq', 'dp'), may hold values from -0.75 to 0.75
- second_moment: float32 [2, 16, 16, 64, 64], P('seq', 'dp'), may hold values from 0.004 to 0.04
Outputs:
- new_left: float32 [2, 16, 16, 64, 64], P('seq', 'dp')
- new_right: float32 [2, 16, 16, 64, 64], P('seq', 'dp')
- direction: float32 [2, 16, 16, 64, 64], P('seq', 'dp')
Inputs may be any that keep to these rules, and one draw needn't show every extreme that they name: `keep_lists`: each row lists 8 different column blocks, and every column block is kept in some row. `left_gram`: each block is symmetric. `right_gram`: each block is symmetric.
All inputs are finite; a program needn't handle non-finite values.
Results may differ from a plain program's by a relative error of at most 0.0003.
Values may be sent and summed in bfloat16 or wider, within the bound.
A program may use at most 64 MiB of HBM per device.

v0:
```python
import jax
import jax.numpy as jnp
from jax import lax
from jax.sharding import PartitionSpec as P

BLOCK = 64


def precondition(gradient, left_gram, right_gram, left_basis, right_basis, second_moment):
    highest = lax.Precision.HIGHEST
    new_left = 0.95 * left_gram + 0.05 * jnp.einsum(
        "...ij,...kj->...ik", gradient, gradient, precision=highest
    )
    new_right = 0.95 * right_gram + 0.05 * jnp.einsum(
        "...ji,...jk->...ik", gradient, gradient, precision=highest
    )
    partial_rot = jnp.einsum("...ji,...jk->...ik", left_basis, gradient, precision=highest)
    rotated = jnp.einsum("...ij,...jk->...ik", partial_rot, right_basis, precision=highest)
    second = 0.95 * second_moment + 0.05 * rotated * rotated
    scaled = rotated / (jnp.sqrt(second) + 1e-08)
    partial_back = jnp.einsum("...ij,...jk->...ik", left_basis, scaled, precision=highest)
    direction = jnp.einsum("...ij,...kj->...ik", partial_back, right_basis, precision=highest)
    return (new_left, new_right, direction)


def per_device(
    acts, upstream, keep_lists, left_gram, right_gram, left_basis, right_basis, second_moment
):
    share_rows = acts.shape[1]
    share_blocks = share_rows // BLOCK
    kept_share = lax.dynamic_slice_in_dim(
        keep_lists, lax.axis_index("seq") * share_blocks, share_blocks, 0
    )
    gathered = lax.all_gather(upstream, "seq", axis=0, tiled=True)
    grad = lax.dot_general(
        acts, gathered, (((0,), (0,)), ((), ())), preferred_element_type=jnp.float32
    )
    tiles = grad.reshape(share_blocks, BLOCK, grad.shape[1] // BLOCK, BLOCK)
    picked = jnp.take_along_axis(tiles, kept_share[:, None, :, None], axis=2)
    packed = picked.transpose(0, 2, 1, 3)
    data_size = lax.axis_size("dp")
    outgoing = packed.reshape(data_size, -1, BLOCK * BLOCK)
    arrived = lax.all_to_all(outgoing, "dp", split_axis=0, concat_axis=0, tiled=True)
    owned_sum = jnp.sum(arrived, axis=0)
    gradient = owned_sum.reshape(1, 1, -1, BLOCK, BLOCK)
    new_left, new_right, direction = precondition(
        gradient, left_gram, right_gram, left_basis, right_basis, second_moment
    )
    return (new_left, new_right, direction)


def solution(mesh):
    in_specs = (
        P("dp", "seq"),
        P(("dp", "seq"), None),
        P(),
        P("seq", "dp", None, None, None),
        P("seq", "dp", None, None, None),
        P("seq", "dp", None, None, None),
        P("seq", "dp", None, None, None),
        P("seq", "dp", None, None, None),
    )
    out_specs = (
        P("seq", "dp", None, None, None),
        P("seq", "dp", None, None, None),
        P("seq", "dp", None, None, None),
    )
    return jax.shard_map(
        per_device, mesh=mesh, in_specs=in_specs, out_specs=out_specs, check_vma=False
    )
```

profile of v0, /device:TPU:0, one launch (start us, length us, event | category | flops | bytes accessed | tf_op | source)
XLA Modules:
  0.0 177.6 jit_solution(2412908082115186528)
XLA Ops:
  0.6 0.0 copy-start
  0.7 0.9 bitcast_or_fusion
  1.5 0.8 compare_and_fusion
  2.3 2.5 %all_gather.3 = bf16[256,1024]{1,0:T(8,128)(2,1)S(1)} all-gather(bf16[128,1024]{1,0:T(8,128)(2,1)} %param.9), channel_id=1, replica_groups=mesh['dp'=16,'seq'=2] {'seq'}, dimensions={0}, use_global_device_ids=true | all-gather | bytes 786432 | tf_op jit(solution)/shard_map/all_gather | solution.py:34
  4.7 0.0 copy-done
  4.7 4.5 %fusion.26 = f32[2048,1024]{1,0:T(8,128)} fusion(bf16[256,2048]{1,0:T(8,128)(2,1)S(1)} %copy-done, bf16[256,1024]{1,0:T(8,128)(2,1)S(1)} %all_gather.3), kind=kOutput, calls=%fused_computation.34 | convolution fusion | flops 1073741824 | bytes 9961472 | tf_op jit(solution)/shard_map/dot_general | solution.py:35
  9.2 13.3 %reshape.70 = f32[32,64,16,64]{3,2,1,0:T(8,128)} reshape(f32[2048,1024]{1,0:T(8,128)} %fusion.26) | data formatting | bytes 16777216 | tf_op jit(solution)/shard_map/reshape | solution.py:38
  22.6 15.8 %copy.17 = f32[32,64,16,64]{3,1,2,0:T(8,128)} copy(f32[32,64,16,64]{3,2,1,0:T(8,128)} %reshape.70) | data formatting | bytes 16777216 | tf_op jit(solution)/shard_map/reshape | solution.py:38
  38.4 0.1 copy.16
  38.5 0.1 reshape.77
  38.6 0.1 copy.15
  38.7 10.2 %gather_fusion = f32[256,64,64]{2,1,0:T(8,128)} fusion(f32[32,64,16,64]{3,1,2,0:T(8,128)} %copy.17, s32[256]{0:T(256)S(1)} %reshape.77), kind=kCustom, calls=%fused_computation | custom fusion | bytes 8390656 | tf_op jit(solution)/shard_map/jit(take_along_axis)/gather | solution.py:39
  48.9 5.8 %broadcast_select_fusion = f32[32,8,64,64]{3,2,1,0:T(8,128)} fusion(f32[32,8,64,64]{3,2,1,0:T(8,128)} %bitcast.57, pred[32,8]{1,0:T(8,128)(4,1)S(1)} %copy.15), kind=kLoop, calls=%fused_computation.1 | loop fusion | flops 1048576 | bytes 8388864 | tf_op jit(solution)/shard_map/jit(take_along_axis)/select_n | solution.py:39
  54.6 7.9 %reshape.72 = f32[16,16,4096]{2,1,0:T(8,128)} reshape(f32[32,8,64,64]{3,2,1,0:T(8,128)} %broadcast_select_fusion) | data formatting | bytes 8388608 | tf_op jit(solution)/shard_map/reshape | solution.py:42
  62.5 0.0 copy-start.4
  62.5 0.0 copy-start.3
  62.5 0.0 copy-start.2
  62.5 0.0 copy-start.1
  62.5 102.5 %all_to_all.5 = f32[16,16,4096]{2,1,0:T(8,128)} all-to-all(f32[16,16,4096]{2,1,0:T(8,128)} %reshape.72), channel_id=1, replica_groups=mesh['dp'=16,'seq'=2] {'dp'}, dimensions={0} | all-to-all | bytes 8388608 | tf_op jit(solution)/shard_map/all_to_all | solution.py:43
  165.1 2.4 %reduce_sum.9 = f32[16,4096]{1,0:T(8,128)S(1)} reduce(f32[16,16,4096]{2,1,0:T(8,128)} %all_to_all.5, f32[]{:T(128)} %constant.30.clone.1), dimensions={0}, to_apply=%region_0.0 | reduce | flops 983040 | bytes 4456452 | tf_op jit(solution)/shard_map/reduce_sum | solution.py:44
  167.5 0.2 reshape.73
  167.7 0.0 copy-done.4
  167.7 1.8 fusion.2
  169.4 2.8 %fusion.3 = f32[1,1,16,64,64]{4,3,2,1,0:T(8,128)} fusion(f32[16,64,64]{2,1,0:T(8,128)S(1)} %reshape.73, f32[1,1,16,64,64]{4,3,2,1,0:T(8,128)} %param.12), kind=kOutput, calls=%fused_computation.8 | convolution fusion | flops 50528256 | bytes 786432 | tf_op jit(solution)/shard_map/...ji,...jk->...ik/dot_general | solution.py:14
  172.3 0.0 copy-done.3
  172.3 1.0 fusion.17
  173.3 0.0 copy-done.2
  173.3 0.6 fusion.14
  174.0 1.9 %fusion.10 = f32[16,64,64]{1,2,0:T(8,128)S(1)} fusion(f32[16,64,64]{2,1,0:T(8,128)S(1)} %fusion.14, f32[1,1,16,64,64]{4,3,2,1,0:T(8,128)S(1)} %copy-done.3, f32[1,1,16,64,64]{4,3,2,1,0:T(8,128)} %param.15), kind=kOutput, calls=%fused_computation.16 | convolution fusion | flops 50724864 | bytes 1048576 | tf_op jit(solution)/shard_map/...ij,...jk->...ik/dot_general | solution.py:21
  175.9 1.8 convolution_bitcast_fusion
  177.6 0.0 copy-done.1
Async XLA Ops:
  0.6 4.1 %copy-start = (bf16[256,2048]{1,0:T(8,128)(2,1)S(1)}, bf16[256,2048]{1,0:T(8,128)(2,1)}, u32[]{:S(2)}) copy-start(bf16[256,2048]{1,0:T(8,128)(2,1)} %param.8) | copy-start | bytes 3145732
  62.5 105.2 %copy-start.4 = (f32[1,1,16,64,64]{4,3,2,1,0:T(8,128)S(1)}, f32[1,1,16,64,64]{4,3,2,1,0:T(8,128)}, u32[]{:S(2)}) copy-start(f32[1,1,16,64,64]{4,3,2,1,0:T(8,128)} %param.11) | copy-start | bytes 786436
  62.5 109.8 %copy-start.3 = (f32[1,1,16,64,64]{4,3,2,1,0:T(8,128)S(1)}, f32[1,1,16,64,64]{4,3,2,1,0:T(8,128)}, u32[]{:S(2)}) copy-start(f32[1,1,16,64,64]{4,3,2,1,0:T(8,128)} %param.13) | copy-start | bytes 786436
  62.5 110.8 %copy-start.2 = (f32[1,1,16,64,64]{4,3,2,1,0:T(8,128)S(1)}, f32[1,1,16,64,64]{4,3,2,1,0:T(8,128)}, u32[]{:S(2)}) copy-start(f32[1,1,16,64,64]{4,3,2,1,0:T(8,128)} %param.14) | copy-start | bytes 786436
  62.5 115.1 %copy-start.1 = (bf16[256,2048]{1,0:T(8,128)(2,1)S(1)}, bf16[256,2048]{1,0:T(8,128)(2,1)}, u32[]{:S(2)}) copy-start(bf16[256,2048]{1,0:T(8,128)(2,1)} %param.8) | copy-start | bytes 3145732
where the time goes:
time: 178 us
  blocking collectives  105 us (59%)
  local copies, waits for them, and re-layouts  47.7 us (27%)
  matrix products  14.4 us (8%)
  other arithmetic  9.79 us (5%)
    all_to_all x1, blocking collectives, per_device(): lax.all_to_all(outgoing, 'dp', split_axis=0, concat_axis=0, tiled=True)  103 us
    reshape x2, local copies, waits for them, and re-layouts, per_device(): tiles = grad.reshape(share_blocks, BLOCK, grad.shape[1] // BLOCK, BLOCK)  29.2 us
    gather x3, local copies, waits for them, and re-layouts, per_device(): picked = jnp.take_along_axis(tiles, kept_share[:, None, :, None], axis=2)  10.3 us
    reshape x1, local copies, waits for them, and re-layouts, per_device(): outgoing = packed.reshape(data_size, -1, BLOCK * BLOCK)  7.89 us
    select_n x1, other arithmetic, per_device(): picked = jnp.take_along_axis(tiles, kept_share[:, None, :, None], axis=2)  5.77 us
    dot_general x1, matrix products, per_device(): lax.dot_general(acts, gathered, (((0,), (0,)), ((), ())), preferred_eleme...  4.51 us

commit v1 on v0

v1 whole, which is shorter than its diff:
```python
import functools

import jax
import jax.numpy as jnp
from jax import lax
from jax.experimental import pallas as pl
from jax.experimental.pallas import tpu as pltpu
from jax.sharding import PartitionSpec as P

BLOCK = 64
LANES = 128
TOP = 32766.0
MESH = pl.DeviceIdType.MESH


def precondition(gradient, left_gram, right_gram, left_basis, right_basis, second_moment):
    highest = lax.Precision.HIGHEST
    new_left = 0.95 * left_gram + 0.05 * jnp.einsum(
        "...ij,...kj->...ik", gradient, gradient, precision=highest
    )
    new_right = 0.95 * right_gram + 0.05 * jnp.einsum(
        "...ji,...jk->...ik", gradient, gradient, precision=highest
    )
    partial_rot = jnp.einsum("...ji,...jk->...ik", left_basis, gradient, precision=highest)
    rotated = jnp.einsum("...ij,...jk->...ik", partial_rot, right_basis, precision=highest)
    second = 0.95 * second_moment + 0.05 * rotated * rotated
    scaled = rotated / (jnp.sqrt(second) + 1e-08)
    partial_back = jnp.einsum("...ij,...jk->...ik", left_basis, scaled, precision=highest)
    direction = jnp.einsum("...ij,...kj->...ik", partial_back, right_basis, precision=highest)
    return (new_left, new_right, direction)


def encode(value):
    peak = jnp.maximum(jnp.max(jnp.abs(value), axis=0, keepdims=True), 1e-30)
    coded = jnp.round(value * (TOP / peak)).astype(jnp.int32).astype(jnp.int16)
    return coded, peak * (1.0 / TOP)


def decode(coded, scale):
    return coded.astype(jnp.int32).astype(jnp.float32) * scale


def reduce_kernel(
    nz, kept, keep_ref, acts_ref, up_ref, out_ref,
    upt, product, acc,
    send1, send2, send3, recv1, recv2, recv3,
    ssend1, ssend2, ssend3, srecv1, srecv2, srecv3,
    up_sems, sems1, sems2, sems3,
):
    dp, seq = lax.axis_index("dp"), lax.axis_index("seq")
    x, y, z = lax.rem(dp, 2), lax.rem(dp // 2, 2), dp // 4
    ox, oy = 1 - x, 1 - y
    x_peer = (z * 2 + y) * 2 + ox
    y_peer = (z * 2 + oy) * 2 + x
    first_peer = (x_peer, y_peer)
    second_peer = (y_peer, x_peer)

    def z_peer(step):
        return (lax.rem(z + step + 1, nz) * 2 + y) * 2 + x

    barrier = pltpu.get_barrier_semaphore()
    pl.semaphore_signal(barrier, inc=1, device_id=(dp, 1 - seq), device_id_type=MESH)
    for peer in (x_peer, y_peer) + tuple(z_peer(step) for step in range(nz - 1)):
        pl.semaphore_signal(barrier, inc=1, device_id=(peer, seq), device_id_type=MESH)
    upt[seq] = up_ref[...].T
    pl.semaphore_wait(barrier, nz + 2)

    def remote(src, dst, sems, peer):
        return pltpu.make_async_remote_copy(
            src_ref=src, dst_ref=dst, send_sem=sems.at[0], recv_sem=sems.at[1],
            device_id=peer, device_id_type=MESH,
        )

    up_copy = remote(upt.at[seq], upt.at[seq], up_sems, (dp, 1 - seq))
    up_copy.start()
    up_copy.wait()

    half_slots = kept // 2
    half_rows = half_slots * BLOCK
    blocks = 2 * (acts_ref.shape[1] // LANES)
    low = lax.broadcasted_iota(jnp.int32, (BLOCK, LANES), 1) < BLOCK

    def copies1(half, step):
        peer = (first_peer[half], seq)
        return (
            remote(send1.at[half, step], recv1.at[half, step], sems1.at[half, step, 0], peer),
            remote(ssend1.at[half, step], srecv1.at[half, step], sems1.at[half, step, 1], peer),
        )

    def copies2(half, step):
        peer = (second_peer[half], seq)
        return (
            remote(send2.at[half, step], recv2.at[half, step], sems2.at[half, step, 0], peer),
            remote(ssend2.at[half, step], srecv2.at[half, step], sems2.at[half, step, 1], peer),
        )

    def copies3(half, step):
        peer = (z_peer(step), seq)
        return (
            remote(send3.at[half, step], recv3.at[half, step], sems3.at[half, step, 0], peer),
            remote(ssend3.at[half, step], srecv3.at[half, step], sems3.at[half, step, 1], peer),
        )

    def produce(step, carry):
        to_z = lax.rem(z + step + 1, nz)
        for dy in range(2):
            base = (to_z * 2 + (y if dy == 0 else oy)) * 2
            columns = pl.ds(pl.multiple_of(base * LANES, 2 * LANES), 2 * LANES)
            whole = jnp.dot(
                jnp.concatenate([upt[0], upt[1]], axis=1),
                acts_ref[:, columns],
                preferred_element_type=jnp.float32,
            )
            product[0] = whole[:, :LANES].reshape(-1, BLOCK, LANES)
            product[1] = whole[:, LANES:].reshape(-1, BLOCK, LANES)
            for dx in range(2):
                to_x = x if dx == 0 else ox
                row_block = seq * blocks + (base + to_x) * 2
                for half in range(2):
                    parts = []
                    for slot in range(half * half_slots, (half + 1) * half_slots):
                        top = keep_ref[row_block * kept + slot]
                        bottom = keep_ref[(row_block + 1) * kept + slot]
                        parts.append(
                            jnp.where(low, product[to_x, top], product[to_x, bottom])
                        )
                    value = jnp.concatenate(parts, axis=0)
                    away, slot = ((dx, dy), (dy, dx))[half]
                    if away:
                        coded, scale = encode(value)
                        send1[half, step, slot] = coded
                        ssend1[half, step, slot] = jnp.broadcast_to(scale, (8, LANES))
                    else:
                        acc[half, step, slot] = value
        for half in range(2):
            for copy in copies1(half, step):
                copy.start()
        return carry

    lax.fori_loop(0, nz, produce, 0)

    for step in range(nz + 1):
        if step < nz:
            for half in range(2):
                for copy in copies1(half, step):
                    copy.wait_recv()
                away = acc[half, step, 1] + decode(
                    recv1[half, step, 1], srecv1[half, step, 1, 0:1, :]
                )
                coded, scale = encode(away)
                send2[half, step] = coded
                ssend2[half, step] = jnp.broadcast_to(scale, (8, LANES))
                for copy in copies2(half, step):
                    copy.start()
                acc[half, step, 0] += decode(
                    recv1[half, step, 0], srecv1[half, step, 0, 0:1, :]
                )
        if step > 0:
            done = step - 1
            for half in range(2):
                for copy in copies2(half, done):
                    copy.wait_recv()
                total = acc[half, done, 0] + decode(
                    recv2[half, done], srecv2[half, done, 0:1, :]
                )
                if done < nz - 1:
                    coded, scale = encode(total)
                    send3[half, done] = coded
                    ssend3[half, done] = jnp.broadcast_to(scale, (8, LANES))
                    for copy in copies3(half, done):
                        copy.start()
                else:
                    acc[half, done, 0] = total

    for half in range(2):
        total = acc[half, nz - 1, 0]
        for step in range(nz - 1):
            for copy in copies3(half, step):
                copy.wait_recv()
            total += decode(recv3[half, step], srecv3[half, step, 0:1, :])
        out_ref[half * half_rows : (half + 1) * half_rows, :] = total

    for half in range(2):
        for step in range(nz):
            for copy in copies1(half, step) + copies2(half, step):
                copy.wait_send()
            if step < nz - 1:
                for copy in copies3(half, step):
                    copy.wait_send()


def reduced_blocks(acts, upstream, keep_lists, nz):
    kept = keep_lists.shape[1]
    half_rows = kept // 2 * BLOCK
    tokens, rows = upstream.shape[0], upstream.shape[1]
    rest = max(nz - 1, 1)
    half = (half_rows, LANES)
    scale = (8, LANES)
    dma = pltpu.SemaphoreType.DMA
    vmem = pl.BlockSpec(memory_space=pltpu.VMEM)
    return pl.pallas_call(
        functools.partial(reduce_kernel, nz, kept),
        out_shape=jax.ShapeDtypeStruct((kept * BLOCK, LANES), jnp.float32),
        in_specs=[pl.BlockSpec(memory_space=pltpu.SMEM), vmem, vmem],
        out_specs=vmem,
        scratch_shapes=[
            pltpu.VMEM((2, rows, tokens), jnp.bfloat16),
            pltpu.VMEM((2, rows // BLOCK, BLOCK, LANES), jnp.float32),
            pltpu.VMEM((2, nz, 2) + half, jnp.float32),
            pltpu.VMEM((2, nz, 2) + half, jnp.int16),
            pltpu.VMEM((2, nz) + half, jnp.int16),
            pltpu.VMEM((2, rest) + half, jnp.int16),
            pltpu.VMEM((2, nz, 2) + half, jnp.int16),
            pltpu.VMEM((2, nz) + half, jnp.int16),
            pltpu.VMEM((2, rest) + half, jnp.int16),
            pltpu.VMEM((2, nz, 2) + scale, jnp.float32),
            pltpu.VMEM((2, nz) + scale, jnp.float32),
            pltpu.VMEM((2, rest) + scale, jnp.float32),
            pltpu.VMEM((2, nz, 2) + scale, jnp.float32),
            pltpu.VMEM((2, nz) + scale, jnp.float32),
            pltpu.VMEM((2, rest) + scale, jnp.float32),
            dma((2,)),
            dma((2, nz, 2, 2)),
            dma((2, nz, 2, 2)),
            dma((2, rest, 2, 2)),
        ],
        compiler_params=pltpu.CompilerParams(
            collective_id=0, has_side_effects=True, vmem_limit_bytes=48 * 1024 * 1024
        ),
        name="reduce_kept",
    )(keep_lists.reshape(-1), acts, upstream)


def per_device(
    acts, upstream, keep_lists, left_gram, right_gram, left_basis, right_basis, second_moment
):
    share_rows = acts.shape[1]
    share_blocks = share_rows // BLOCK
    kept = keep_lists.shape[1]
    data_size = lax.axis_size("dp")
    fits = (
        lax.axis_size("seq") == 2
        and data_size % 4 == 0
        and share_rows == data_size * LANES
        and kept % 2 == 0
        and upstream.shape[0] % LANES == 0
    )
    if fits:
        arrived = reduced_blocks(acts, upstream, keep_lists, data_size // 4)
        tiles = arrived.reshape(kept, BLOCK, LANES // BLOCK, BLOCK)
        gradient = tiles.transpose(2, 0, 3, 1).reshape(1, 1, -1, BLOCK, BLOCK)
    else:
        kept_share = lax.dynamic_slice_in_dim(
            keep_lists, lax.axis_index("seq") * share_blocks, share_blocks, 0
        )
        gathered = lax.all_gather(upstream, "seq", axis=0, tiled=True)
        grad = lax.dot_general(
            acts, gathered, (((0,), (0,)), ((), ())), preferred_element_type=jnp.float32
        )
        tiles = grad.reshape(share_blocks, BLOCK, grad.shape[1] // BLOCK, BLOCK)
        picked = jnp.take_along_axis(tiles, kept_share[:, None, :, None], axis=2)
        outgoing = picked.transpose(0, 2, 1, 3).reshape(data_size, -1, BLOCK * BLOCK)
        owned_sum = lax.psum_scatter(outgoing, "dp", scatter_dimension=0)
        gradient = owned_sum.reshape(1, 1, -1, BLOCK, BLOCK)
    return precondition(
        gradient, left_gram, right_gram, left_basis, right_basis, second_moment
    )


def solution(mesh):
    block = P("seq", "dp", None, None, None)
    return jax.shard_map(
        per_device,
        mesh=mesh,
        in_specs=(P("dp", "seq"), P(("dp", "seq"), None), P()) + (block,) * 5,
        out_specs=(block,) * 3,
        check_vma=False,
    )
```

time: 178 us -> 50.3 us (0.28)
  blocking collectives: 105 us -> 0 us
  local copies, waits for them, and re-layouts: 47.7 us -> 4.87 us
  Pallas kernels: 0 us -> 35.9 us
  other arithmetic: 9.79 us -> 0 us
  matrix products: 14.4 us -> 7.84 us
    all_to_all x1 -> x0, blocking collectives: 103 us -> none  [per_device(): lax.all_to_all(outgoing, 'dp', split_axis=0, concat_axis=0, tiled=True)]
    reshape x3, local copies, waits for them, and re-layouts: 37.1 us -> 0.46 us  [the longest x1 0.32 us: per_device(): tiles = arrived.reshape(kept, BLOCK, LANES // BLOCK, BLOCK)]
    pallas_call x0 -> x1, Pallas kernels: none -> 35.9 us  [reduced_blocks(): pl.pallas_call(functools.partial(reduce_kernel, nz, kept), out_shape=jax....]
    gather x3 -> x0, local copies, waits for them, and re-layouts: 10.3 us -> none  [per_device(): picked = jnp.take_along_axis(tiles, kept_share[:, None, :, None], axis=2)]
    select_n x1 -> x0, other arithmetic: 5.77 us -> none  [per_device(): picked = jnp.take_along_axis(tiles, kept_share[:, None, :, None], axis=2)]
    dot_general x1 -> x0, matrix products: 4.51 us -> none  [per_device(): lax.dot_general(acts, gathered, (((0,), (0,)), ((), ())), preferred_eleme...]
    unnamed x10 -> x15, local copies, waits for them, and re-layouts: 0.03 us -> 4.41 us
    all_gather x1 -> x0, blocking collectives: 2.46 us -> none  [per_device(): gathered = lax.all_gather(upstream, 'seq', axis=0, tiled=True)]
where the time goes in v1:
time: 50.3 us; the launch traced here: 49.3 us
  Pallas kernels  35.9 us (71%)
  matrix products  7.84 us (16%)
  local copies, waits for them, and re-layouts  4.87 us (10%)
  between operations  0.7 us (1%)
    pallas_call x1, Pallas kernels, reduced_blocks(): pl.pallas_call(functools.partial(reduce_kernel, nz, kept), out_shape=jax....  35.9 us
    unnamed x15, local copies, waits for them, and re-layouts  4.41 us
    dot_general x1, matrix products, precondition(): jnp.einsum('...ij,...kj->...ik', gradient, gradient, precision=highest)  1.8 us
    dot_general x1, matrix products, precondition(): jnp.einsum('...ij,...kj->...ik', partial_back, right_basis, precision=hig...  1.76 us
    dot_general x1, matrix products, precondition(): jnp.einsum('...ji,...jk->...ik', gradient, gradient, precision=highest)  1.75 us
    dot_general x1, matrix products, precondition(): jnp.einsum('...ji,...jk->...ik', left_basis, gradient, precision=highest)  1.02 us

profile of v1, /device:TPU:0, one launch (start us, length us, event | category | flops | bytes accessed | tf_op | source)
XLA Modules:
  0.0 49.3 jit_solution(15275890983319310776)
XLA Ops:
  0.6 0.0 copy-start
  0.6 0.8 %copy.15 = s32[64,8]{1,0:T(8,128)S(1)} copy(s32[64,8]{0,1:T(8,128)} %param.10) | data formatting | bytes 4096 | tf_op args[2]
  1.5 0.1 reshape.50.keep_ref
  1.6 0.0 copy-start.1
  1.6 1.2 %copy-done.1 = bf16[256,2048]{1,0:T(8,128)(2,1)S(1)} copy-done((bf16[256,2048]{1,0:T(8,128)(2,1)S(1)}, bf16[256,2048]{1,0:T(8,128)(2,1)}, u32[]{:S(2)}) %copy-start.1) | copy-done | bytes 1048600
  2.8 0.0 copy-start.2
  2.8 0.9 %copy-done.2 = bf16[128,1024]{1,0:T(8,128)(2,1)S(1)} copy-done((bf16[128,1024]{1,0:T(8,128)(2,1)S(1)}, bf16[128,1024]{1,0:T(8,128)(2,1)}, u32[]{:S(2)}) %copy-start.2) | copy-done | bytes 262168
  3.7 35.9 %reduce_kept.1 = f32[512,128]{1,0:T(8,128)S(1)} custom-call(s32[512]{0:T(512)S(1)} %reshape.50.keep_ref, bf16[256,2048]{1,0:T(8,128)(2,1)S(1)} %copy-done.1, bf16[128,1024]{1,0:T(8,128)(2,1)S(1)} %copy-done.2), custom_call_target="tpu_custom_call" | custom-call | tf_op jit(solution)/shard_map/reduce_kept/pallas_call | solution.py:201
  39.6 0.3 reshape.51
  40.0 0.0 copy-start.4
  40.0 0.1 copy.24
  40.0 1.0 %copy-done.4 = f32[1,1,16,64,64]{4,3,2,1,0:T(8,128)S(1)} copy-done((f32[1,1,16,64,64]{4,3,2,1,0:T(8,128)S(1)}, f32[1,1,16,64,64]{4,3,2,1,0:T(8,128)}, u32[]{:S(2)}) %copy-start.4) | copy-done | bytes 262168
  41.0 1.8 %fusion.3 = f32[1,1,16,64,64]{4,3,2,1,0:T(8,128)} fusion(f32[16,64,64]{1,2,0:T(8,128)S(1)} %bitcast.56, f32[1,1,16,64,64]{4,3,2,1,0:T(8,128)S(1)} %copy-done.4), kind=kOutput, calls=%fused_computation.6 | convolution fusion | flops 50528256 | bytes 786432 | tf_op jit(solution)/shard_map/...ji,...jk->...ik/dot_general | solution.py:21
  42.8 0.0 copy-done
  42.8 0.0 copy-start.5
  42.8 1.0 %fusion.17 = f32[16,64,64]{1,2,0:T(8,128)S(1)} fusion(f32[16,64,64]{1,2,0:T(8,128)S(1)} %bitcast.57, f32[1,1,16,64,64]{4,3,2,1,0:T(8,128)S(1)} %copy-done), kind=kOutput, calls=%fused_computation.20 | convolution fusion | flops 50331648 | bytes 786432 | tf_op jit(solution)/shard_map/...ji,...jk->...ik/dot_general | solution.py:24
  43.8 0.0 copy-done.5
  43.8 0.0 copy-start.3
  43.8 1.8 %fusion.2 = f32[1,1,16,64,64]{4,3,2,1,0:T(8,128)} fusion(f32[16,64,64]{1,2,0:T(8,128)S(1)} %bitcast.58, f32[1,1,16,64,64]{4,3,2,1,0:T(8,128)S(1)} %copy-done.5), kind=kOutput, calls=%fused_computation.5 | convolution fusion | flops 50528256 | bytes 786432 | tf_op jit(solution)/shard_map/...ij,...kj->...ik/dot_general | solution.py:18
  45.6 0.0 copy-done.3
  45.6 0.0 copy-start.6
  45.6 0.6 %fusion.14 = f32[16,64,64]{2,1,0:T(8,128)S(1)} fusion(f32[16,64,64]{1,2,0:T(8,128)S(1)} %fusion.17, f32[1,1,16,64,64]{4,3,2,1,0:T(8,128)S(1)} %copy-done.3), kind=kOutput, calls=%fused_computation.17 | convolution fusion | flops 50331648 | bytes 786432 | tf_op jit(solution)/shard_map/...ij,...jk->...ik/dot_general | solution.py:25
  46.3 0.4 copy-done.6
  46.7 0.9 %fusion.10 = f32[16,64,64]{1,2,0:T(8,128)S(1)} fusion(f32[16,64,64]{2,1,0:T(8,128)S(1)} %fusion.14, f32[1,1,16,64,64]{4,3,2,1,0:T(8,128)S(1)} %copy-done, f32[1,1,16,64,64]{4,3,2,1,0:T(8,128)S(1)} %copy-done.6), kind=kOutput, calls=%fused_computation.14 | convolution fusion | flops 50724864 | bytes 1048576 | tf_op jit(solution)/shard_map/...ij,...jk->...ik/dot_general | solution.py:28
  47.5 1.8 %convolution_bitcast_fusion = f32[1,1,16,64,64]{4,3,2,1,0:T(8,128)} fusion(f32[16,64,64]{1,2,0:T(8,128)S(1)} %fusion.10, f32[1,1,16,64,64]{4,3,2,1,0:T(8,128)S(1)} %copy-done.3), kind=kOutput, calls=%fused_computation.4 | convolution fusion | flops 50331648 | bytes 786432 | tf_op jit(solution)/shard_map/...ij,...kj->...ik/dot_general | solution.py:29
Async XLA Ops:
  0.6 42.1 %copy-start = (f32[1,1,16,64,64]{4,3,2,1,0:T(8,128)S(1)}, f32[1,1,16,64,64]{4,3,2,1,0:T(8,128)}, u32[]{:S(2)}) copy-start(f32[1,1,16,64,64]{4,3,2,1,0:T(8,128)} %param.13) | copy-start | bytes 786436
  1.6 1.2 %copy-start.1 = (bf16[256,2048]{1,0:T(8,128)(2,1)S(1)}, bf16[256,2048]{1,0:T(8,128)(2,1)}, u32[]{:S(2)}) copy-start(bf16[256,2048]{1,0:T(8,128)(2,1)} %acts_ref.1) | copy-start | bytes 3145732
  2.8 0.9 %copy-start.2 = (bf16[128,1024]{1,0:T(8,128)(2,1)S(1)}, bf16[128,1024]{1,0:T(8,128)(2,1)}, u32[]{:S(2)}) copy-start(bf16[128,1024]{1,0:T(8,128)(2,1)} %up_ref.1) | copy-start | bytes 786436
  40.0 1.0 %copy-start.4 = (f32[1,1,16,64,64]{4,3,2,1,0:T(8,128)S(1)}, f32[1,1,16,64,64]{4,3,2,1,0:T(8,128)}, u32[]{:S(2)}) copy-start(f32[1,1,16,64,64]{4,3,2,1,0:T(8,128)} %param.12) | copy-start | bytes 786436
  42.8 1.0 %copy-start.5 = (f32[1,1,16,64,64]{4,3,2,1,0:T(8,128)S(1)}, f32[1,1,16,64,64]{4,3,2,1,0:T(8,128)}, u32[]{:S(2)}) copy-start(f32[1,1,16,64,64]{4,3,2,1,0:T(8,128)} %param.11) | copy-start | bytes 786436
  43.8 1.8 %copy-start.3 = (f32[1,1,16,64,64]{4,3,2,1,0:T(8,128)S(1)}, f32[1,1,16,64,64]{4,3,2,1,0:T(8,128)}, u32[]{:S(2)}) copy-start(f32[1,1,16,64,64]{4,3,2,1,0:T(8,128)} %param.14) | copy-start | bytes 786436
  45.6 1.0 %copy-start.6 = (f32[1,1,16,64,64]{4,3,2,1,0:T(8,128)S(1)}, f32[1,1,16,64,64]{4,3,2,1,0:T(8,128)}, u32[]{:S(2)}) copy-start(f32[1,1,16,64,64]{4,3,2,1,0:T(8,128)} %param.15) | copy-start | bytes 786436

commit v2 on v1

--- a/solution.py
+++ b/solution.py
@@ -41,11 +41,11 @@
 
 
 def reduce_kernel(
-    nz, kept, keep_ref, acts_ref, up_ref, out_ref,
-    upt, product, acc,
+    nz, kept, keep_ref, acts_hbm, up_hbm, out_ref,
+    acts, up, upt, product, acc,
     send1, send2, send3, recv1, recv2, recv3,
     ssend1, ssend2, ssend3, srecv1, srecv2, srecv3,
-    up_sems, sems1, sems2, sems3,
+    load_sems, up_sems, sems1, sems2, sems3,
 ):
     dp, seq = lax.axis_index("dp"), lax.axis_index("seq")
     x, y, z = lax.rem(dp, 2), lax.rem(dp // 2, 2), dp // 4
@@ -55,14 +55,32 @@
     first_peer = (x_peer, y_peer)
     second_peer = (y_peer, x_peer)
 
+    def z_target(step):
+        last = step // max(nz - 1, 1)
+        return lax.rem(z + (1 - last) * (lax.rem(step + nz // 2 - 1, max(nz - 1, 1)) + 1), nz)
+
     def z_peer(step):
-        return (lax.rem(z + step + 1, nz) * 2 + y) * 2 + x
+        return (z_target(step) * 2 + y) * 2 + x
+
+    width = 4 * LANES
+
+    def load(step):
+        columns = pl.ds(pl.multiple_of(z_target(step) * width, width), width)
+        return pltpu.make_async_copy(
+            acts_hbm.at[:, columns], acts.at[step], load_sems.at[step + 1]
+        )
+
+    up_load = pltpu.make_async_copy(up_hbm, up, load_sems.at[0])
+    up_load.start()
+    for step in range(nz):
+        load(step).start()
 
     barrier = pltpu.get_barrier_semaphore()
     pl.semaphore_signal(barrier, inc=1, device_id=(dp, 1 - seq), device_id_type=MESH)
     for peer in (x_peer, y_peer) + tuple(z_peer(step) for step in range(nz - 1)):
         pl.semaphore_signal(barrier, inc=1, device_id=(peer, seq), device_id_type=MESH)
-    upt[seq] = up_ref[...].T
+    up_load.wait()
+    upt[seq] = up[...].T
     pl.semaphore_wait(barrier, nz + 2)
 
     def remote(src, dst, sems, peer):
@@ -77,7 +95,7 @@
 
     half_slots = kept // 2
     half_rows = half_slots * BLOCK
-    blocks = 2 * (acts_ref.shape[1] // LANES)
+    blocks = 8 * nz
     low = lax.broadcasted_iota(jnp.int32, (BLOCK, LANES), 1) < BLOCK
 
     def copies1(half, step):
@@ -101,26 +119,26 @@
             remote(ssend3.at[half, step], srecv3.at[half, step], sems3.at[half, step, 1], peer),
         )
 
-    def produce(step, carry):
-        to_z = lax.rem(z + step + 1, nz)
-        for dy in range(2):
-            base = (to_z * 2 + (y if dy == 0 else oy)) * 2
-            columns = pl.ds(pl.multiple_of(base * LANES, 2 * LANES), 2 * LANES)
+    def produce(step):
+        load(step).wait()
+        for dy in (1, 0):
+            to_y = y if dy == 0 else oy
+            columns = pl.ds(pl.multiple_of(to_y * (2 * LANES), 2 * LANES), 2 * LANES)
             whole = jnp.dot(
                 jnp.concatenate([upt[0], upt[1]], axis=1),
-                acts_ref[:, columns],
+                acts[step, :, columns],
                 preferred_element_type=jnp.float32,
             )
             product[0] = whole[:, :LANES].reshape(-1, BLOCK, LANES)
             product[1] = whole[:, LANES:].reshape(-1, BLOCK, LANES)
-            for dx in range(2):
+            for dx in (1, 0):
                 to_x = x if dx == 0 else ox
-                row_block = seq * blocks + (base + to_x) * 2
+                row_block = seq * blocks + ((z_target(step) * 2 + to_y) * 2 + to_x) * 2
                 for half in range(2):
                     parts = []
                     for slot in range(half * half_slots, (half + 1) * half_slots):
-                        top = keep_ref[row_block * kept + slot]
-                        bottom = keep_ref[(row_block + 1) * kept + slot]
+                        top = keep_ref[row_block, slot]
+                        bottom = keep_ref[row_block + 1, slot]
                         parts.append(
                             jnp.where(low, product[to_x, top], product[to_x, bottom])
                         )
@@ -132,48 +150,55 @@
                         ssend1[half, step, slot] = jnp.broadcast_to(scale, (8, LANES))
                     else:
                         acc[half, step, slot] = value
-        for half in range(2):
+            for copy in copies1(dy, step):
+                copy.start()
+
+    def forward(step):
+        for half in (1, 0):
             for copy in copies1(half, step):
+                copy.wait_recv()
+            away = acc[half, step, 1] + decode(
+                recv1[half, step, 1], srecv1[half, step, 1, 0:1, :]
+            )
+            coded, scale = encode(away)
+            send2[half, step] = coded
+            ssend2[half, step] = jnp.broadcast_to(scale, (8, LANES))
+            for copy in copies2(half, step):
                 copy.start()
+            acc[half, step, 0] += decode(recv1[half, step, 0], srecv1[half, step, 0, 0:1, :])
+
+    def settle(step, half):
+        for copy in copies2(half, step):
+            copy.wait_recv()
+        return acc[half, step, 0] + decode(recv2[half, step], srecv2[half, step, 0:1, :])
+
+    def spread(step):
+        for half in (1, 0):
+            coded, scale = encode(settle(step, half))
+            send3[half, step] = coded
+            ssend3[half, step] = jnp.broadcast_to(scale, (8, LANES))
+            for copy in copies3(half, step):
+                copy.start()
+
+    def turn(step, carry):
+        @pl.when(step < nz)
+        def _():
+            produce(step)
+
+        @pl.when((step >= 1) & (step <= nz))
+        def _():
+            forward(step - 1)
+
+        @pl.when(step >= 2)
+        def _():
+            spread(step - 2)
+
         return carry
 
-    lax.fori_loop(0, nz, produce, 0)
-
-    for step in range(nz + 1):
-        if step < nz:
-            for half in range(2):
-                for copy in copies1(half, step):
-                    copy.wait_recv()
-                away = acc[half, step, 1] + decode(
-                    recv1[half, step, 1], srecv1[half, step, 1, 0:1, :]
-                )
-                coded, scale = encode(away)
-                send2[half, step] = coded
-                ssend2[half, step] = jnp.broadcast_to(scale, (8, LANES))
-                for copy in copies2(half, step):
-                    copy.start()
-                acc[half, step, 0] += decode(
-                    recv1[half, step, 0], srecv1[half, step, 0, 0:1, :]
-                )
-        if step > 0:
-            done = step - 1
-            for half in range(2):
-                for copy in copies2(half, done):
-                    copy.wait_recv()
-                total = acc[half, done, 0] + decode(
-                    recv2[half, done], srecv2[half, done, 0:1, :]
-                )
-                if done < nz - 1:
-                    coded, scale = encode(total)
-                    send3[half, done] = coded
-                    ssend3[half, done] = jnp.broadcast_to(scale, (8, LANES))
-                    for copy in copies3(half, done):
-                        copy.start()
-                else:
-                    acc[half, done, 0] = total
+    lax.fori_loop(0, nz + 1, turn, 0)
 
     for half in range(2):
-        total = acc[half, nz - 1, 0]
+        total = settle(nz - 1, half)
         for step in range(nz - 1):
             for copy in copies3(half, step):
                 copy.wait_recv()
@@ -197,13 +222,15 @@
     half = (half_rows, LANES)
     scale = (8, LANES)
     dma = pltpu.SemaphoreType.DMA
-    vmem = pl.BlockSpec(memory_space=pltpu.VMEM)
+    vmem, hbm = (pl.BlockSpec(memory_space=space) for space in (pltpu.VMEM, pl.ANY))
     return pl.pallas_call(
         functools.partial(reduce_kernel, nz, kept),
         out_shape=jax.ShapeDtypeStruct((kept * BLOCK, LANES), jnp.float32),
-        in_specs=[pl.BlockSpec(memory_space=pltpu.SMEM), vmem, vmem],
+        in_specs=[pl.BlockSpec(memory_space=pltpu.SMEM), hbm, hbm],
         out_specs=vmem,
         scratch_shapes=[
+            pltpu.VMEM((nz, acts.shape[0], 4 * LANES), jnp.bfloat16),
+            pltpu.VMEM(upstream.shape, jnp.bfloat16),
             pltpu.VMEM((2, rows, tokens), jnp.bfloat16),
             pltpu.VMEM((2, rows // BLOCK, BLOCK, LANES), jnp.float32),
             pltpu.VMEM((2, nz, 2) + half, jnp.float32),
@@ -219,16 +246,17 @@
             pltpu.VMEM((2, nz, 2) + scale, jnp.float32),
             pltpu.VMEM((2, nz) + scale, jnp.float32),
             pltpu.VMEM((2, rest) + scale, jnp.float32),
+            dma((nz + 1,)),
             dma((2,)),
             dma((2, nz, 2, 2)),
             dma((2, nz, 2, 2)),
             dma((2, rest, 2, 2)),
         ],
         compiler_params=pltpu.CompilerParams(
-            collective_id=0, has_side_effects=True, vmem_limit_bytes=48 * 1024 * 1024
+            collective_id=0, has_side_effects=True, vmem_limit_bytes=24 * 1024 * 1024
         ),
         name="reduce_kept",
-    )(keep_lists.reshape(-1), acts, upstream)
+    )(keep_lists, acts, upstream)
 
 
 def per_device(

time: 50.3 us -> 47.5 us (0.944); the launches traced: 49.3 us -> 47.1 us
  Pallas kernels: 35.9 us -> 33.8 us
    pallas_call x1, Pallas kernels: 35.9 us -> 33.8 us  [reduced_blocks(): pl.pallas_call(functools.partial(reduce_kernel, nz, kept), out_shape=jax....]
where the time goes in v2:
time: 47.5 us; the launch traced here: 47.1 us
  Pallas kernels  33.8 us (71%)
  matrix products  7.84 us (17%)
  local copies, waits for them, and re-layouts  4.78 us (10%)
  between operations  0.69 us (1%)
    pallas_call x1, Pallas kernels, reduced_blocks(): pl.pallas_call(functools.partial(reduce_kernel, nz, kept), out_shape=jax....  33.8 us
    unnamed x15, local copies, waits for them, and re-layouts  4.41 us
    dot_general x1, matrix products, precondition(): jnp.einsum('...ij,...kj->...ik', gradient, gradient, precision=highest)  1.8 us
    dot_general x1, matrix products, precondition(): jnp.einsum('...ij,...kj->...ik', partial_back, right_basis, precision=hig...  1.76 us
    dot_general x1, matrix products, precondition(): jnp.einsum('...ji,...jk->...ik', gradient, gradient, precision=highest)  1.75 us
    dot_general x1, matrix products, precondition(): jnp.einsum('...ji,...jk->...ik', left_basis, gradient, precision=highest)  1.02 us

profile of v2, /device:TPU:0, one launch (start us, length us, event | category | flops | bytes accessed | tf_op | source)
XLA Modules:
  0.0 47.1 jit_solution(4493359891430698005)
XLA Ops:
  0.6 0.0 copy-start
  0.6 0.8 %copy.11.keep_ref = s32[64,8]{1,0:T(8,128)S(1)} copy(s32[64,8]{0,1:T(8,128)} %param.10) | data formatting | bytes 4096 | tf_op args[2]
  1.5 0.0 copy-start.1
  1.5 1.2 %copy-done.1 = bf16[256,2048]{1,0:T(8,128)(2,1)S(1)} copy-done((bf16[256,2048]{1,0:T(8,128)(2,1)S(1)}, bf16[256,2048]{1,0:T(8,128)(2,1)}, u32[]{:S(2)}) %copy-start.1) | copy-done | bytes 1048600
  2.7 0.0 copy-start.2
  2.7 0.9 %copy-done.2 = bf16[128,1024]{1,0:T(8,128)(2,1)S(1)} copy-done((bf16[128,1024]{1,0:T(8,128)(2,1)S(1)}, bf16[128,1024]{1,0:T(8,128)(2,1)}, u32[]{:S(2)}) %copy-start.2) | copy-done | bytes 262168
  3.6 33.8 %reduce_kept.1 = f32[512,128]{1,0:T(8,128)S(1)} custom-call(s32[64,8]{1,0:T(8,128)S(1)} %copy.11.keep_ref, bf16[256,2048]{1,0:T(8,128)(2,1)S(1)} %copy-done.1, bf16[128,1024]{1,0:T(8,128)(2,1)S(1)} %copy-done.2), custom_call_target="tpu_custom_call" | custom-call | tf_op jit(solution)/shard_map/reduce_kept/pallas_call | solution.py:226
  37.5 0.3 reshape.47
  37.8 0.0 copy-start.4
  37.8 0.1 copy.20
  37.9 1.0 %copy-done.4 = f32[1,1,16,64,64]{4,3,2,1,0:T(8,128)S(1)} copy-done((f32[1,1,16,64,64]{4,3,2,1,0:T(8,128)S(1)}, f32[1,1,16,64,64]{4,3,2,1,0:T(8,128)}, u32[]{:S(2)}) %copy-start.4) | copy-done | bytes 262168
  38.9 1.7 %fusion.3 = f32[1,1,16,64,64]{4,3,2,1,0:T(8,128)} fusion(f32[16,64,64]{1,2,0:T(8,128)S(1)} %bitcast.56, f32[1,1,16,64,64]{4,3,2,1,0:T(8,128)S(1)} %copy-done.4), kind=kOutput, calls=%fused_computation.6 | convolution fusion | flops 50528256 | bytes 786432 | tf_op jit(solution)/shard_map/...ji,...jk->...ik/dot_general | solution.py:21
  40.6 0.0 copy-done
  40.6 0.0 copy-start.5
  40.6 1.0 %fusion.17 = f32[16,64,64]{1,2,0:T(8,128)S(1)} fusion(f32[16,64,64]{1,2,0:T(8,128)S(1)} %bitcast.57, f32[1,1,16,64,64]{4,3,2,1,0:T(8,128)S(1)} %copy-done), kind=kOutput, calls=%fused_computation.20 | convolution fusion | flops 50331648 | bytes 786432 | tf_op jit(solution)/shard_map/...ji,...jk->...ik/dot_general | solution.py:24
  41.6 0.0 copy-done.5
  41.7 0.0 copy-start.3
  41.7 1.8 %fusion.2 = f32[1,1,16,64,64]{4,3,2,1,0:T(8,128)} fusion(f32[16,64,64]{1,2,0:T(8,128)S(1)} %bitcast.58, f32[1,1,16,64,64]{4,3,2,1,0:T(8,128)S(1)} %copy-done.5), kind=kOutput, calls=%fused_computation.5 | convolution fusion | flops 50528256 | bytes 786432 | tf_op jit(solution)/shard_map/...ij,...kj->...ik/dot_general | solution.py:18
  43.5 0.0 copy-done.3
  43.5 0.0 copy-start.6
  43.5 0.6 %fusion.14 = f32[16,64,64]{2,1,0:T(8,128)S(1)} fusion(f32[16,64,64]{1,2,0:T(8,128)S(1)} %fusion.17, f32[1,1,16,64,64]{4,3,2,1,0:T(8,128)S(1)} %copy-done.3), kind=kOutput, calls=%fused_computation.17 | convolution fusion | flops 50331648 | bytes 786432 | tf_op jit(solution)/shard_map/...ij,...jk->...ik/dot_general | solution.py:25
  44.1 0.4 copy-done.6
  44.5 0.9 %fusion.10 = f32[16,64,64]{1,2,0:T(8,128)S(1)} fusion(f32[16,64,64]{2,1,0:T(8,128)S(1)} %fusion.14, f32[1,1,16,64,64]{4,3,2,1,0:T(8,128)S(1)} %copy-done, f32[1,1,16,64,64]{4,3,2,1,0:T(8,128)S(1)} %copy-done.6), kind=kOutput, calls=%fused_computation.14 | convolution fusion | flops 50724864 | bytes 1048576 | tf_op jit(solution)/shard_map/...ij,...jk->...ik/dot_general | solution.py:28
  45.4 1.8 %convolution_bitcast_fusion = f32[1,1,16,64,64]{4,3,2,1,0:T(8,128)} fusion(f32[16,64,64]{1,2,0:T(8,128)S(1)} %fusion.10, f32[1,1,16,64,64]{4,3,2,1,0:T(8,128)S(1)} %copy-done.3), kind=kOutput, calls=%fused_computation.4 | convolution fusion | flops 50331648 | bytes 786432 | tf_op jit(solution)/shard_map/...ij,...kj->...ik/dot_general | solution.py:29
Async XLA Ops:
  0.6 40.0 %copy-start = (f32[1,1,16,64,64]{4,3,2,1,0:T(8,128)S(1)}, f32[1,1,16,64,64]{4,3,2,1,0:T(8,128)}, u32[]{:S(2)}) copy-start(f32[1,1,16,64,64]{4,3,2,1,0:T(8,128)} %param.13) | copy-start | bytes 786436
  1.5 1.2 %copy-start.1 = (bf16[256,2048]{1,0:T(8,128)(2,1)S(1)}, bf16[256,2048]{1,0:T(8,128)(2,1)}, u32[]{:S(2)}) copy-start(bf16[256,2048]{1,0:T(8,128)(2,1)} %acts_hbm.1) | copy-start | bytes 3145732
  2.7 0.9 %copy-start.2 = (bf16[128,1024]{1,0:T(8,128)(2,1)S(1)}, bf16[128,1024]{1,0:T(8,128)(2,1)}, u32[]{:S(2)}) copy-start(bf16[128,1024]{1,0:T(8,128)(2,1)} %up_hbm.1) | copy-start | bytes 786436
  37.8 1.0 %copy-start.4 = (f32[1,1,16,64,64]{4,3,2,1,0:T(8,128)S(1)}, f32[1,1,16,64,64]{4,3,2,1,0:T(8,128)}, u32[]{:S(2)}) copy-start(f32[1,1,16,64,64]{4,3,2,1,0:T(8,128)} %param.12) | copy-start | bytes 786436
  40.6 1.0 %copy-start.5 = (f32[1,1,16,64,64]{4,3,2,1,0:T(8,128)S(1)}, f32[1,1,16,64,64]{4,3,2,1,0:T(8,128)}, u32[]{:S(2)}) copy-start(f32[1,1,16,64,64]{4,3,2,1,0:T(8,128)} %param.11) | copy-start | bytes 786436
  41.7 1.8 %copy-start.3 = (f32[1,1,16,64,64]{4,3,2,1,0:T(8,128)S(1)}, f32[1,1,16,64,64]{4,3,2,1,0:T(8,128)}, u32[]{:S(2)}) copy-start(f32[1,1,16,64,64]{4,3,2,1,0:T(8,128)} %param.14) | copy-start | bytes 786436
  43.5 1.0 %copy-start.6 = (f32[1,1,16,64,64]{4,3,2,1,0:T(8,128)S(1)}, f32[1,1,16,64,64]{4,3,2,1,0:T(8,128)}, u32[]{:S(2)}) copy-start(f32[1,1,16,64,64]{4,3,2,1,0:T(8,128)} %param.15) | copy-start | bytes 786436

commit v3 on v2

--- a/solution.py
+++ b/solution.py
@@ -137,8 +137,8 @@
                 for half in range(2):
                     parts = []
                     for slot in range(half * half_slots, (half + 1) * half_slots):
-                        top = keep_ref[row_block, slot]
-                        bottom = keep_ref[row_block + 1, slot]
+                        top = keep_ref[slot, row_block]
+                        bottom = keep_ref[slot, row_block + 1]
                         parts.append(
                             jnp.where(low, product[to_x, top], product[to_x, bottom])
                         )
@@ -222,7 +222,7 @@
     half = (half_rows, LANES)
     scale = (8, LANES)
     dma = pltpu.SemaphoreType.DMA
-    vmem, hbm = (pl.BlockSpec(memory_space=space) for space in (pltpu.VMEM, pl.ANY))
+    vmem, hbm = (pl.BlockSpec(memory_space=space) for space in (pltpu.VMEM, pltpu.HBM))
     return pl.pallas_call(
         functools.partial(reduce_kernel, nz, kept),
         out_shape=jax.ShapeDtypeStruct((kept * BLOCK, LANES), jnp.float32),
@@ -255,8 +255,65 @@
         compiler_params=pltpu.CompilerParams(
             collective_id=0, has_side_effects=True, vmem_limit_bytes=24 * 1024 * 1024
         ),
+        cost_estimate=pl.CostEstimate(
+            flops=2 * acts.size * rows,
+            bytes_accessed=16 * (acts.size + upstream.size),
+            transcendentals=0,
+        ),
         name="reduce_kept",
-    )(keep_lists, acts, upstream)
+    )(keep_lists.T, acts, upstream)
+
+
+NN = (((1,), (0,)), ((), ()))
+NT = (((1,), (1,)), ((), ()))
+
+
+def split(value):
+    high = value.astype(jnp.bfloat16)
+    return high, (value - high.astype(jnp.float32)).astype(jnp.bfloat16)
+
+
+def product3(left, right, dims):
+    dot = functools.partial(
+        lax.dot_general, dimension_numbers=dims, preferred_element_type=jnp.float32
+    )
+    (lh, ll), (rh, rl) = left, right
+    return dot(lh, rh) + (dot(lh, rl) + dot(ll, rh))
+
+
+def states_kernel(
+    kept, grad_ref, left_gram, right_gram, left_basis, right_basis, moment,
+    new_left, new_right, direction,
+):
+    for slot in range(kept):
+        across = grad_ref[slot * BLOCK : (slot + 1) * BLOCK, :]
+        down = across.T
+        for part in range(LANES // BLOCK):
+            at = (0, 0, part * kept + slot)
+            span = slice(part * BLOCK, (part + 1) * BLOCK)
+            block, turned = split(down[span, :]), split(across[:, span])
+            left, right = left_basis[at], right_basis[at]
+            left2, right2 = split(left), split(right)
+            new_left[at] = 0.95 * left_gram[at] + 0.05 * product3(block, block, NT)
+            new_right[at] = 0.95 * right_gram[at] + 0.05 * product3(turned, turned, NT)
+            partial_rot = product3(split(left.T), block, NN)
+            rotated = product3(split(partial_rot), right2, NN)
+            second = 0.95 * moment[at] + 0.05 * rotated * rotated
+            scaled = rotated / (jnp.sqrt(second) + 1e-08)
+            partial_back = product3(left2, split(scaled), NN)
+            direction[at] = product3(split(partial_back), right2, NT)
+
+
+def update_states(arrived, left_gram, right_gram, left_basis, right_basis, second_moment):
+    vmem = pl.BlockSpec(memory_space=pltpu.VMEM)
+    return pl.pallas_call(
+        functools.partial(states_kernel, arrived.shape[0] // BLOCK),
+        out_shape=(jax.ShapeDtypeStruct(left_gram.shape, jnp.float32),) * 3,
+        in_specs=[vmem] * 6,
+        out_specs=(vmem,) * 3,
+        compiler_params=pltpu.CompilerParams(vmem_limit_bytes=16 * 1024 * 1024),
+        name="update_states",
+    )(arrived, left_gram, right_gram, left_basis, right_basis, second_moment)
 
 
 def per_device(
@@ -275,8 +332,9 @@
     )
     if fits:
         arrived = reduced_blocks(acts, upstream, keep_lists, data_size // 4)
-        tiles = arrived.reshape(kept, BLOCK, LANES // BLOCK, BLOCK)
-        gradient = tiles.transpose(2, 0, 3, 1).reshape(1, 1, -1, BLOCK, BLOCK)
+        return update_states(
+            arrived, left_gram, right_gram, left_basis, right_basis, second_moment
+        )
     else:
         kept_share = lax.dynamic_slice_in_dim(
             keep_lists, lax.axis_index("seq") * share_blocks, share_blocks, 0

time: 47.5 us -> 44.5 us (0.937)
  matrix products: 7.84 us -> 0 us
  Pallas kernels: 33.8 us -> 40.7 us
  local copies, waits for them, and re-layouts: 4.78 us -> 2.87 us
    dot_general x6 -> x0, matrix products: 7.84 us -> none  [the longest x1 1.8 us: precondition(): jnp.einsum('...ij,...kj->...ik', gradient, gradient, precision=highest)]
    pallas_call x0 -> x1, Pallas kernels: none -> 7.37 us  [update_states(): pl.pallas_call(functools.partial(states_kernel, arrived.shape[0] // BLOCK...]
    unnamed x15 -> x16, local copies, waits for them, and re-layouts: 4.41 us -> 2.87 us
where the time goes in v3:
time: 44.5 us; the launch traced here: 44.3 us
  Pallas kernels  40.7 us (91%)
  local copies, waits for them, and re-layouts  2.87 us (6%)
  between operations  0.7 us (2%)
    pallas_call x1, Pallas kernels, reduced_blocks(): pl.pallas_call(functools.partial(reduce_kernel, nz, kept), out_shape=jax....  33.4 us
    pallas_call x1, Pallas kernels, update_states(): pl.pallas_call(functools.partial(states_kernel, arrived.shape[0] // BLOCK...  7.37 us
    unnamed x16, local copies, waits for them, and re-layouts  2.87 us

profile of v3, /device:TPU:0, one launch (start us, length us, event | category | flops | bytes accessed | tf_op | source)
XLA Modules:
  0.0 44.3 jit_solution(4658478818121429055)
XLA Ops:
  0.6 0.0 copy-start.5
  0.6 1.2 %copy-done.5 = bf16[256,2048]{1,0:T(8,128)(2,1)S(1)} copy-done((bf16[256,2048]{1,0:T(8,128)(2,1)S(1)}, bf16[256,2048]{1,0:T(8,128)(2,1)}, u32[]{:S(2)}) %copy-start.5) | copy-done | bytes 1048600
  1.9 0.0 copy-start.6
  1.9 0.9 %copy-done.6 = bf16[128,1024]{1,0:T(8,128)(2,1)S(1)} copy-done((bf16[128,1024]{1,0:T(8,128)(2,1)S(1)}, bf16[128,1024]{1,0:T(8,128)(2,1)}, u32[]{:S(2)}) %copy-start.6) | copy-done | bytes 262168
  2.8 0.0 copy-start.7
  2.8 0.7 %copy-done.7 = s32[64,8]{0,1:T(8,128)S(1)} copy-done((s32[64,8]{0,1:T(8,128)S(1)}, s32[64,8]{0,1:T(8,128)}, u32[]{:S(2)}) %copy-start.7) | copy-done | bytes 2072
  3.5 0.0 copy-start
  3.5 0.0 copy-start.1
  3.5 0.0 copy-start.2
  3.5 0.0 copy-start.3
  3.5 0.0 copy-start.4
  3.5 33.4 %reduce_kept.1.grad_ref = f32[512,128]{1,0:T(8,128)S(1)} custom-call(s32[8,64]{1,0:T(8,128)S(1)} %bitcast.1, bf16[256,2048]{1,0:T(8,128)(2,1)S(1)} %copy-done.5, bf16[128,1024]{1,0:T(8,128)(2,1)S(1)} %copy-done.6), custom_call_target="tpu_custom_call" | custom-call | flops 1073741824 | bytes 10485760 | tf_op jit(solution)/shard_map/reduce_kept/pallas_call | solution.py:226
  36.9 0.0 copy-done
  36.9 0.0 copy-done.1
  36.9 0.0 copy-done.2
  36.9 0.0 copy-done.3
  36.9 0.0 copy-done.4
  36.9 7.4 %update_states.1 = (f32[1,1,16,64,64]{4,3,2,1,0:T(8,128)}, f32[1,1,16,64,64]{4,3,2,1,0:T(8,128)}, f32[1,1,16,64,64]{4,3,2,1,0:T(8,128)}) custom-call(f32[512,128]{1,0:T(8,128)S(1)} %reduce_kept.1.grad_ref, f32[1,1,16,64,64]{4,3,2,1,0:T(8,128)S(1)} %copy-done, f32[1,1,16,64,64]{4,3,2,1,0:T(8,128)S(1)} %copy-done.1, f32[1,1,16,64,64]{4,3,2,1,0:T(8,128)S(1)} %copy-done.2, ...), custom_call_target="tpu_custom_call" | custom-call | tf_op jit(solution)/shard_map/update_states/pallas_call | solution.py:309
Async XLA Ops:
  0.6 1.2 %copy-start.5 = (bf16[256,2048]{1,0:T(8,128)(2,1)S(1)}, bf16[256,2048]{1,0:T(8,128)(2,1)}, u32[]{:S(2)}) copy-start(bf16[256,2048]{1,0:T(8,128)(2,1)} %acts_hbm.1) | copy-start | bytes 3145732
  1.9 0.9 %copy-start.6 = (bf16[128,1024]{1,0:T(8,128)(2,1)S(1)}, bf16[128,1024]{1,0:T(8,128)(2,1)}, u32[]{:S(2)}) copy-start(bf16[128,1024]{1,0:T(8,128)(2,1)} %up_hbm.1) | copy-start | bytes 786436
  2.8 0.7 %copy-start.7 = (s32[64,8]{0,1:T(8,128)S(1)}, s32[64,8]{0,1:T(8,128)}, u32[]{:S(2)}) copy-start(s32[64,8]{0,1:T(8,128)} %param.10) | copy-start | bytes 6148
  3.5 33.4 %copy-start = (f32[1,1,16,64,64]{4,3,2,1,0:T(8,128)S(1)}, f32[1,1,16,64,64]{4,3,2,1,0:T(8,128)}, u32[]{:S(2)}) copy-start(f32[1,1,16,64,64]{4,3,2,1,0:T(8,128)} %left_gram.1) | copy-start | bytes 786436
  3.5 33.4 %copy-start.1 = (f32[1,1,16,64,64]{4,3,2,1,0:T(8,128)S(1)}, f32[1,1,16,64,64]{4,3,2,1,0:T(8,128)}, u32[]{:S(2)}) copy-start(f32[1,1,16,64,64]{4,3,2,1,0:T(8,128)} %right_gram.1) | copy-start | bytes 786436
  3.5 33.4 %copy-start.2 = (f32[1,1,16,64,64]{4,3,2,1,0:T(8,128)S(1)}, f32[1,1,16,64,64]{4,3,2,1,0:T(8,128)}, u32[]{:S(2)}) copy-start(f32[1,1,16,64,64]{4,3,2,1,0:T(8,128)} %left_basis.1) | copy-start | bytes 786436
  3.5 33.4 %copy-start.3 = (f32[1,1,16,64,64]{4,3,2,1,0:T(8,128)S(1)}, f32[1,1,16,64,64]{4,3,2,1,0:T(8,128)}, u32[]{:S(2)}) copy-start(f32[1,1,16,64,64]{4,3,2,1,0:T(8,128)} %right_basis.1) | copy-start | bytes 786436
  3.5 33.4 %copy-start.4 = (f32[1,1,16,64,64]{4,3,2,1,0:T(8,128)S(1)}, f32[1,1,16,64,64]{4,3,2,1,0:T(8,128)}, u32[]{:S(2)}) copy-start(f32[1,1,16,64,64]{4,3,2,1,0:T(8,128)} %moment.1) | copy-start | bytes 786436

commit v4 on v2

--- a/solution.py
+++ b/solution.py
@@ -40,12 +40,88 @@
     return coded.astype(jnp.int32).astype(jnp.float32) * scale
 
 
+def split(value):
+    high = value.astype(jnp.bfloat16)
+    return high, (value - high.astype(jnp.float32)).astype(jnp.bfloat16)
+
+
+def stacked(left, right):
+    out = jnp.dot(left, right, preferred_element_type=jnp.float32)
+    rows, columns = out.shape[0] // 2, out.shape[1] // 2
+    return out[:rows, :columns] + (out[:rows, columns:] + out[rows:, :columns])
+
+
+def rows_of(value):
+    return jnp.concatenate(split(value), axis=0)
+
+
+def beside(value):
+    return jnp.concatenate(split(value), axis=1)
+
+
+def diagonal(pair, low):
+    return jnp.concatenate([jnp.where(low, pair, 0.0), jnp.where(low, 0.0, pair)], axis=0)
+
+
+def own_halves(value, low):
+    return jnp.where(low, value[:BLOCK], value[BLOCK:])
+
+
+def prepare(slot, kept, low, states, ready):
+    _, _, left_basis, right_basis, moment = states
+    left_by, left_turned, right_rows, right_turned, moment_turned = ready
+    pair = (slot, kept + slot)
+    left = jnp.concatenate([left_basis[at] for at in pair], axis=1)
+    left_by[slot] = beside(diagonal(left, low))
+    left_t = jnp.concatenate([left_basis[at].T for at in pair], axis=1)
+    left_turned[slot] = beside(diagonal(left_t, low))
+    right_rows[slot] = rows_of(jnp.concatenate([right_basis[at] for at in pair], axis=0))
+    right_turned[slot] = rows_of(jnp.concatenate([right_basis[at].T for at in pair], axis=0))
+    moment_turned[slot] = jnp.concatenate([moment[at].T for at in pair], axis=1)
+
+
+def update(slots, blocks, kept, low, states, ready, outs):
+    left_gram, right_gram = states[:2]
+    left_by, left_turned, right_rows, right_turned, moment_turned = ready
+    new_left, new_right, direction = outs
+    parts = (slice(0, BLOCK), slice(BLOCK, LANES))
+    partial = [stacked(rows_of(t), left_by[k]) for k, t in zip(slots, blocks)]
+    turned = [t.T for t in blocks]
+    rotated = [
+        own_halves(stacked(right_turned[k], beside(p)), low) for k, p in zip(slots, partial)
+    ]
+    scaled = [
+        r / (jnp.sqrt(0.95 * moment_turned[k] + 0.05 * r * r) + 1e-08)
+        for k, r in zip(slots, rotated)
+    ]
+    back = [stacked(rows_of(v), left_turned[k]) for k, v in zip(slots, scaled)]
+    for k, t, u in zip(slots, blocks, turned):
+        outer = stacked(rows_of(u), beside(t))
+        masked = split(jnp.concatenate([jnp.where(low, t, 0.0), jnp.where(low, 0.0, t)], axis=0))
+        halves = split(u)
+        dot = functools.partial(jnp.dot, preferred_element_type=jnp.float32)
+        inner = dot(masked[0], halves[0]) + (
+            dot(masked[0], halves[1]) + dot(masked[1], halves[0])
+        )
+        for part, span in enumerate(parts):
+            at = part * kept + k
+            new_left[0, 0, at] = 0.95 * left_gram[at] + 0.05 * outer[span, span]
+            new_right[0, 0, at] = 0.95 * right_gram[at] + 0.05 * inner[span]
+    for k, q in zip(slots, back):
+        result = own_halves(stacked(right_rows[k], beside(q)), low).T
+        for part, span in enumerate(parts):
+            direction[0, 0, part * kept + k] = result[span]
+
+
 def reduce_kernel(
-    nz, kept, keep_ref, acts_hbm, up_hbm, out_ref,
-    acts, up, upt, product, acc,
+    nz, kept, keep_ref, acts_hbm, up_hbm,
+    left_gram, right_gram, left_basis, right_basis, moment,
+    new_left, new_right, direction,
+    acts, up, upt, product, acc, states,
+    left_by, left_turned, right_rows, right_turned, moment_turned,
     send1, send2, send3, recv1, recv2, recv3,
     ssend1, ssend2, ssend3, srecv1, srecv2, srecv3,
-    load_sems, up_sems, sems1, sems2, sems3,
+    load_sems, state_sems, up_sems, sems1, sems2, sems3,
 ):
     dp, seq = lax.axis_index("dp"), lax.axis_index("seq")
     x, y, z = lax.rem(dp, 2), lax.rem(dp // 2, 2), dp // 4
@@ -75,6 +151,15 @@
     for step in range(nz):
         load(step).start()
 
+    state_loads = [
+        pltpu.make_async_copy(ref.at[0, 0], states.at[i], state_sems.at[i])
+        for i, ref in enumerate((left_gram, right_gram, left_basis, right_basis, moment))
+    ]
+    for state_load in state_loads:
+        state_load.start()
+    held = tuple(states.at[i] for i in range(len(state_loads)))
+    ready = (left_by, left_turned, right_rows, right_turned, moment_turned)
+
     barrier = pltpu.get_barrier_semaphore()
     pl.semaphore_signal(barrier, inc=1, device_id=(dp, 1 - seq), device_id_type=MESH)
     for peer in (x_peer, y_peer) + tuple(z_peer(step) for step in range(nz - 1)):
@@ -94,7 +179,6 @@
     up_copy.wait()
 
     half_slots = kept // 2
-    half_rows = half_slots * BLOCK
     blocks = 8 * nz
     low = lax.broadcasted_iota(jnp.int32, (BLOCK, LANES), 1) < BLOCK
 
@@ -137,8 +221,8 @@
                 for half in range(2):
                     parts = []
                     for slot in range(half * half_slots, (half + 1) * half_slots):
-                        top = keep_ref[row_block, slot]
-                        bottom = keep_ref[row_block + 1, slot]
+                        top = keep_ref[slot, row_block]
+                        bottom = keep_ref[slot, row_block + 1]
                         parts.append(
                             jnp.where(low, product[to_x, top], product[to_x, bottom])
                         )
@@ -185,7 +269,14 @@
         def _():
             produce(step)
 
-        @pl.when((step >= 1) & (step <= nz))
+        @pl.when(step == 1)
+        def _():
+            for state_load in state_loads:
+                state_load.wait()
+            for slot in range(kept):
+                prepare(slot, kept, low, held, ready)
+
+        @pl.when(step >= 1)
         def _():
             forward(step - 1)
 
@@ -197,13 +288,17 @@
 
     lax.fori_loop(0, nz + 1, turn, 0)
 
-    for half in range(2):
+    for half in (1, 0):
         total = settle(nz - 1, half)
         for step in range(nz - 1):
             for copy in copies3(half, step):
                 copy.wait_recv()
             total += decode(recv3[half, step], srecv3[half, step, 0:1, :])
-        out_ref[half * half_rows : (half + 1) * half_rows, :] = total
+        update(
+            tuple(range(half * half_slots, (half + 1) * half_slots)),
+            [total[i * BLOCK : (i + 1) * BLOCK] for i in range(half_slots)],
+            kept, low, held, ready, (new_left, new_right, direction),
+        )
 
     for half in range(2):
         for step in range(nz):
@@ -214,7 +309,7 @@
                     copy.wait_send()
 
 
-def reduced_blocks(acts, upstream, keep_lists, nz):
+def fused_step(acts, upstream, keep_lists, states, nz):
     kept = keep_lists.shape[1]
     half_rows = kept // 2 * BLOCK
     tokens, rows = upstream.shape[0], upstream.shape[1]
@@ -222,18 +317,24 @@
     half = (half_rows, LANES)
     scale = (8, LANES)
     dma = pltpu.SemaphoreType.DMA
-    vmem, hbm = (pl.BlockSpec(memory_space=space) for space in (pltpu.VMEM, pl.ANY))
+    vmem, hbm = (pl.BlockSpec(memory_space=space) for space in (pltpu.VMEM, pltpu.HBM))
     return pl.pallas_call(
         functools.partial(reduce_kernel, nz, kept),
-        out_shape=jax.ShapeDtypeStruct((kept * BLOCK, LANES), jnp.float32),
-        in_specs=[pl.BlockSpec(memory_space=pltpu.SMEM), hbm, hbm],
-        out_specs=vmem,
+        out_shape=(jax.ShapeDtypeStruct(states[0].shape, jnp.float32),) * 3,
+        in_specs=[pl.BlockSpec(memory_space=pltpu.SMEM)] + [hbm] * (2 + len(states)),
+        out_specs=(vmem,) * 3,
         scratch_shapes=[
             pltpu.VMEM((nz, acts.shape[0], 4 * LANES), jnp.bfloat16),
             pltpu.VMEM(upstream.shape, jnp.bfloat16),
             pltpu.VMEM((2, rows, tokens), jnp.bfloat16),
             pltpu.VMEM((2, rows // BLOCK, BLOCK, LANES), jnp.float32),
             pltpu.VMEM((2, nz, 2) + half, jnp.float32),
+            pltpu.VMEM((len(states),) + states[0].shape[2:], jnp.float32),
+            pltpu.VMEM((kept, LANES, 2 * LANES), jnp.bfloat16),
+            pltpu.VMEM((kept, LANES, 2 * LANES), jnp.bfloat16),
+            pltpu.VMEM((kept, 2 * LANES, BLOCK), jnp.bfloat16),
+            pltpu.VMEM((kept, 2 * LANES, BLOCK), jnp.bfloat16),
+            pltpu.VMEM((kept, BLOCK, LANES), jnp.float32),
             pltpu.VMEM((2, nz, 2) + half, jnp.int16),
             pltpu.VMEM((2, nz) + half, jnp.int16),
             pltpu.VMEM((2, rest) + half, jnp.int16),
@@ -247,16 +348,22 @@
             pltpu.VMEM((2, nz) + scale, jnp.float32),
             pltpu.VMEM((2, rest) + scale, jnp.float32),
             dma((nz + 1,)),
+            dma((len(states),)),
             dma((2,)),
             dma((2, nz, 2, 2)),
             dma((2, nz, 2, 2)),
             dma((2, rest, 2, 2)),
         ],
         compiler_params=pltpu.CompilerParams(
-            collective_id=0, has_side_effects=True, vmem_limit_bytes=24 * 1024 * 1024
+            collective_id=0, has_side_effects=True, vmem_limit_bytes=60 * 1024 * 1024
         ),
-        name="reduce_kept",
-    )(keep_lists, acts, upstream)
+        cost_estimate=pl.CostEstimate(
+            flops=2 * acts.size * rows,
+            bytes_accessed=16 * (acts.size + upstream.size),
+            transcendentals=0,
+        ),
+        name="fused_step",
+    )(keep_lists.T, acts, upstream, *states)
 
 
 def per_device(
@@ -274,9 +381,8 @@
         and upstream.shape[0] % LANES == 0
     )
     if fits:
-        arrived = reduced_blocks(acts, upstream, keep_lists, data_size // 4)
-        tiles = arrived.reshape(kept, BLOCK, LANES // BLOCK, BLOCK)
-        gradient = tiles.transpose(2, 0, 3, 1).reshape(1, 1, -1, BLOCK, BLOCK)
+        states = (left_gram, right_gram, left_basis, right_basis, second_moment)
+        return fused_step(acts, upstream, keep_lists, states, data_size // 4)
     else:
         kept_share = lax.dynamic_slice_in_dim(
             keep_lists, lax.axis_index("seq") * share_blocks, share_blocks, 0

time: 47.5 us -> 40.9 us (0.86)
  matrix products: 7.84 us -> 0 us
  Pallas kernels: 33.8 us -> 36 us
  local copies, waits for them, and re-layouts: 4.78 us -> 3.97 us
    dot_general x6 -> x0, matrix products: 7.84 us -> none  [the longest x1 1.8 us: precondition(): jnp.einsum('...ij,...kj->...ik', gradient, gradient, precision=highest)]
    pallas_call x1, Pallas kernels: 33.8 us -> 36 us  [fused_step(): pl.pallas_call(functools.partial(reduce_kernel, nz, kept), out_shape=(jax...]
    unnamed x15 -> x7, local copies, waits for them, and re-layouts: 4.41 us -> 3.97 us
where the time goes in v4:
time: 40.9 us; the launch traced here: 40.6 us
  Pallas kernels  36 us (88%)
  local copies, waits for them, and re-layouts  3.97 us (10%)
  between operations  0.65 us (2%)
    pallas_call x1, Pallas kernels, fused_step(): pl.pallas_call(functools.partial(reduce_kernel, nz, kept), out_shape=(jax...  36 us
    unnamed x7, local copies, waits for them, and re-layouts  3.97 us

profile of v4, /device:TPU:0, one launch (start us, length us, event | category | flops | bytes accessed | tf_op | source)
XLA Modules:
  0.0 40.6 jit_solution(1842800190298611331)
XLA Ops:
  0.6 36.0 %fused_step.1 = (f32[1,1,16,64,64]{4,3,2,1,0:T(8,128)}, f32[1,1,16,64,64]{4,3,2,1,0:T(8,128)}, f32[1,1,16,64,64]{4,3,2,1,0:T(8,128)}) custom-call(s32[8,64]{1,0:T(8,128)} %bitcast.1, bf16[256,2048]{1,0:T(8,128)(2,1)} %acts_hbm.1, bf16[128,1024]{1,0:T(8,128)(2,1)} %up_hbm.1, f32[1,1,16,64,64]{4,3,2,1,0:T(8,128)} %left_gram.1, ...), custom_call_target="tpu_custom_call" | custom-call | flops 1073741824 | bytes 10485760 | tf_op jit(solution)/shard_map/fused_step/pallas_call | solution.py:321
  36.7 0.0 copy-start.1
  36.7 1.9 %copy.14 = f32[1,1,16,64,64]{4,3,2,1,0:T(8,128)} copy(f32[1,1,16,64,64]{4,3,2,1,0:T(8,128)} %get-tuple-element.6) | data formatting | bytes 524288
  38.6 0.0 copy-done.1
  38.6 0.0 copy-start
  38.6 0.8 %copy.15 = f32[1,1,16,64,64]{4,3,2,1,0:T(8,128)} copy(f32[1,1,16,64,64]{4,3,2,1,0:T(8,128)S(1)} %copy-done.1) | data formatting | bytes 524288
  39.4 0.4 %copy-done = f32[1,1,16,64,64]{4,3,2,1,0:T(8,128)S(1)} copy-done((f32[1,1,16,64,64]{4,3,2,1,0:T(8,128)S(1)}, f32[1,1,16,64,64]{4,3,2,1,0:T(8,128)}, u32[]{:S(2)}) %copy-start) | copy-done | bytes 262168
  39.8 0.8 %copy.16 = f32[1,1,16,64,64]{4,3,2,1,0:T(8,128)} copy(f32[1,1,16,64,64]{4,3,2,1,0:T(8,128)S(1)} %copy-done) | data formatting | bytes 524288
Async XLA Ops:
  36.7 2.0 %copy-start.1 = (f32[1,1,16,64,64]{4,3,2,1,0:T(8,128)S(1)}, f32[1,1,16,64,64]{4,3,2,1,0:T(8,128)}, u32[]{:S(2)}) copy-start(f32[1,1,16,64,64]{4,3,2,1,0:T(8,128)} %get-tuple-element.7) | copy-start | bytes 786436
  38.6 1.2 %copy-start = (f32[1,1,16,64,64]{4,3,2,1,0:T(8,128)S(1)}, f32[1,1,16,64,64]{4,3,2,1,0:T(8,128)}, u32[]{:S(2)}) copy-start(f32[1,1,16,64,64]{4,3,2,1,0:T(8,128)} %get-tuple-element.8) | copy-start | bytes 786436

commit v5 on v4

--- a/solution.py
+++ b/solution.py
@@ -10,6 +10,7 @@
 BLOCK = 64
 LANES = 128
 TOP = 32766.0
+GRANT = 65000 * 1024
 MESH = pl.DeviceIdType.MESH
 
 
@@ -132,24 +133,25 @@
     second_peer = (y_peer, x_peer)
 
     def z_target(step):
-        last = step // max(nz - 1, 1)
-        return lax.rem(z + (1 - last) * (lax.rem(step + nz // 2 - 1, max(nz - 1, 1)) + 1), nz)
+        turn_z = step // 2
+        last = turn_z // max(nz - 1, 1)
+        return lax.rem(z + (1 - last) * (lax.rem(turn_z + nz // 2 - 1, max(nz - 1, 1)) + 1), nz)
 
     def z_peer(step):
         return (z_target(step) * 2 + y) * 2 + x
 
     width = 4 * LANES
 
-    def load(step):
-        columns = pl.ds(pl.multiple_of(z_target(step) * width, width), width)
+    def load(turn_z):
+        columns = pl.ds(pl.multiple_of(z_target(2 * turn_z) * width, width), width)
         return pltpu.make_async_copy(
-            acts_hbm.at[:, columns], acts.at[step], load_sems.at[step + 1]
+            acts_hbm.at[:, columns], acts.at[turn_z], load_sems.at[turn_z + 1]
         )
 
     up_load = pltpu.make_async_copy(up_hbm, up, load_sems.at[0])
     up_load.start()
-    for step in range(nz):
-        load(step).start()
+    for turn_z in range(nz):
+        load(turn_z).start()
 
     state_loads = [
         pltpu.make_async_copy(ref.at[0, 0], states.at[i], state_sems.at[i])
@@ -162,7 +164,7 @@
 
     barrier = pltpu.get_barrier_semaphore()
     pl.semaphore_signal(barrier, inc=1, device_id=(dp, 1 - seq), device_id_type=MESH)
-    for peer in (x_peer, y_peer) + tuple(z_peer(step) for step in range(nz - 1)):
+    for peer in (x_peer, y_peer) + tuple(z_peer(2 * turn_z) for turn_z in range(nz - 1)):
         pl.semaphore_signal(barrier, inc=1, device_id=(peer, seq), device_id_type=MESH)
     up_load.wait()
     upt[seq] = up[...].T
@@ -179,6 +181,8 @@
     up_copy.wait()
 
     half_slots = kept // 2
+    run = half_slots // 2
+    steps = 2 * nz
     blocks = 8 * nz
     low = lax.broadcasted_iota(jnp.int32, (BLOCK, LANES), 1) < BLOCK
 
@@ -203,37 +207,42 @@
             remote(ssend3.at[half, step], srecv3.at[half, step], sems3.at[half, step, 1], peer),
         )
 
-    def produce(step):
-        load(step).wait()
+    def multiply(turn_z):
+        load(turn_z).wait()
         for dy in (1, 0):
             to_y = y if dy == 0 else oy
             columns = pl.ds(pl.multiple_of(to_y * (2 * LANES), 2 * LANES), 2 * LANES)
             whole = jnp.dot(
                 jnp.concatenate([upt[0], upt[1]], axis=1),
-                acts[step, :, columns],
+                acts[turn_z, :, columns],
                 preferred_element_type=jnp.float32,
             )
-            product[0] = whole[:, :LANES].reshape(-1, BLOCK, LANES)
-            product[1] = whole[:, LANES:].reshape(-1, BLOCK, LANES)
+            product[dy, 0] = whole[:, :LANES].reshape(-1, BLOCK, LANES)
+            product[dy, 1] = whole[:, LANES:].reshape(-1, BLOCK, LANES)
+
+    def produce(step):
+        for dy in (1, 0):
+            to_y = y if dy == 0 else oy
             for dx in (1, 0):
                 to_x = x if dx == 0 else ox
                 row_block = seq * blocks + ((z_target(step) * 2 + to_y) * 2 + to_x) * 2
                 for half in range(2):
                     parts = []
-                    for slot in range(half * half_slots, (half + 1) * half_slots):
+                    for i in range(run):
+                        slot = half * half_slots + lax.rem(step, 2) * run + i
                         top = keep_ref[slot, row_block]
                         bottom = keep_ref[slot, row_block + 1]
                         parts.append(
-                            jnp.where(low, product[to_x, top], product[to_x, bottom])
+                            jnp.where(low, product[dy, to_x, top], product[dy, to_x, bottom])
                         )
                     value = jnp.concatenate(parts, axis=0)
-                    away, slot = ((dx, dy), (dy, dx))[half]
+                    away, place = ((dx, dy), (dy, dx))[half]
                     if away:
                         coded, scale = encode(value)
-                        send1[half, step, slot] = coded
-                        ssend1[half, step, slot] = jnp.broadcast_to(scale, (8, LANES))
+                        send1[half, step, place] = coded
+                        ssend1[half, step, place] = jnp.broadcast_to(scale, (8, LANES))
                     else:
-                        acc[half, step, slot] = value
+                        acc[half, step, place] = value
             for copy in copies1(dy, step):
                 copy.start()
 
@@ -265,7 +274,11 @@
                 copy.start()
 
     def turn(step, carry):
-        @pl.when(step < nz)
+        @pl.when((step < steps) & (lax.rem(step, 2) == 0))
+        def _():
+            multiply(step // 2)
+
+        @pl.when(step < steps)
         def _():
             produce(step)
 
@@ -273,48 +286,51 @@
         def _():
             for state_load in state_loads:
                 state_load.wait()
-            for slot in range(kept):
-                prepare(slot, kept, low, held, ready)
 
         @pl.when(step >= 1)
         def _():
+            for i in range(kept // steps):
+                prepare((step - 1) * (kept // steps) + i, kept, low, held, ready)
             forward(step - 1)
 
-        @pl.when(step >= 2)
+        @pl.when((step >= 2) & (step < steps))
         def _():
             spread(step - 2)
 
         return carry
 
-    lax.fori_loop(0, nz + 1, turn, 0)
-
-    for half in (1, 0):
-        total = settle(nz - 1, half)
-        for step in range(nz - 1):
-            for copy in copies3(half, step):
-                copy.wait_recv()
-            total += decode(recv3[half, step], srecv3[half, step, 0:1, :])
+    lax.fori_loop(0, steps + 1, turn, 0)
+
+    for odd in range(2):
+        slots, blocks_done = [], []
+        for half in (1, 0):
+            total = settle(steps - 2 + odd, half)
+            for step in range(odd, steps - 2, 2):
+                for copy in copies3(half, step):
+                    copy.wait_recv()
+                total += decode(recv3[half, step], srecv3[half, step, 0:1, :])
+            for i in range(run):
+                slots.append(half * half_slots + odd * run + i)
+                blocks_done.append(total[i * BLOCK : (i + 1) * BLOCK])
         update(
-            tuple(range(half * half_slots, (half + 1) * half_slots)),
-            [total[i * BLOCK : (i + 1) * BLOCK] for i in range(half_slots)],
-            kept, low, held, ready, (new_left, new_right, direction),
+            slots, blocks_done, kept, low, held, ready, (new_left, new_right, direction)
         )
 
     for half in range(2):
-        for step in range(nz):
+        for step in range(steps):
             for copy in copies1(half, step) + copies2(half, step):
                 copy.wait_send()
-            if step < nz - 1:
+            if step < steps - 2:
                 for copy in copies3(half, step):
                     copy.wait_send()
 
 
 def fused_step(acts, upstream, keep_lists, states, nz):
     kept = keep_lists.shape[1]
-    half_rows = kept // 2 * BLOCK
     tokens, rows = upstream.shape[0], upstream.shape[1]
-    rest = max(nz - 1, 1)
-    half = (half_rows, LANES)
+    steps = 2 * nz
+    rest = max(steps - 2, 1)
+    half = (kept // 4 * BLOCK, LANES)
     scale = (8, LANES)
     dma = pltpu.SemaphoreType.DMA
     vmem, hbm = (pl.BlockSpec(memory_space=space) for space in (pltpu.VMEM, pltpu.HBM))
@@ -327,35 +343,35 @@
             pltpu.VMEM((nz, acts.shape[0], 4 * LANES), jnp.bfloat16),
             pltpu.VMEM(upstream.shape, jnp.bfloat16),
             pltpu.VMEM((2, rows, tokens), jnp.bfloat16),
-            pltpu.VMEM((2, rows // BLOCK, BLOCK, LANES), jnp.float32),
-            pltpu.VMEM((2, nz, 2) + half, jnp.float32),
+            pltpu.VMEM((2, 2, rows // BLOCK, BLOCK, LANES), jnp.float32),
+            pltpu.VMEM((2, steps, 2) + half, jnp.float32),
             pltpu.VMEM((len(states),) + states[0].shape[2:], jnp.float32),
             pltpu.VMEM((kept, LANES, 2 * LANES), jnp.bfloat16),
             pltpu.VMEM((kept, LANES, 2 * LANES), jnp.bfloat16),
             pltpu.VMEM((kept, 2 * LANES, BLOCK), jnp.bfloat16),
             pltpu.VMEM((kept, 2 * LANES, BLOCK), jnp.bfloat16),
             pltpu.VMEM((kept, BLOCK, LANES), jnp.float32),
-            pltpu.VMEM((2, nz, 2) + half, jnp.int16),
-            pltpu.VMEM((2, nz) + half, jnp.int16),
+            pltpu.VMEM((2, steps, 2) + half, jnp.int16),
+            pltpu.VMEM((2, steps) + half, jnp.int16),
             pltpu.VMEM((2, rest) + half, jnp.int16),
-            pltpu.VMEM((2, nz, 2) + half, jnp.int16),
-            pltpu.VMEM((2, nz) + half, jnp.int16),
+            pltpu.VMEM((2, steps, 2) + half, jnp.int16),
+            pltpu.VMEM((2, steps) + half, jnp.int16),
             pltpu.VMEM((2, rest) + half, jnp.int16),
-            pltpu.VMEM((2, nz, 2) + scale, jnp.float32),
-            pltpu.VMEM((2, nz) + scale, jnp.float32),
+            pltpu.VMEM((2, steps, 2) + scale, jnp.float32),
+            pltpu.VMEM((2, steps) + scale, jnp.float32),
             pltpu.VMEM((2, rest) + scale, jnp.float32),
-            pltpu.VMEM((2, nz, 2) + scale, jnp.float32),
-            pltpu.VMEM((2, nz) + scale, jnp.float32),
+            pltpu.VMEM((2, steps, 2) + scale, jnp.float32),
+            pltpu.VMEM((2, steps) + scale, jnp.float32),
             pltpu.VMEM((2, rest) + scale, jnp.float32),
             dma((nz + 1,)),
             dma((len(states),)),
             dma((2,)),
-            dma((2, nz, 2, 2)),
-            dma((2, nz, 2, 2)),
+            dma((2, steps, 2, 2)),
+            dma((2, steps, 2, 2)),
             dma((2, rest, 2, 2)),
         ],
         compiler_params=pltpu.CompilerParams(
-            collective_id=0, has_side_effects=True, vmem_limit_bytes=60 * 1024 * 1024
+            collective_id=0, has_side_effects=True, vmem_limit_bytes=GRANT
         ),
         cost_estimate=pl.CostEstimate(
             flops=2 * acts.size * rows,
@@ -364,6 +380,31 @@
         ),
         name="fused_step",
     )(keep_lists.T, acts, upstream, *states)
+
+
+def move_kernel(*refs):
+    count = len(refs) // 2
+    sems = refs[-1]
+    copies = [
+        pltpu.make_async_copy(refs[i], refs[count + i], sems.at[i]) for i in range(count)
+    ]
+    for copy in copies:
+        copy.start()
+    for copy in copies:
+        copy.wait()
+
+
+def moved(arrays):
+    anywhere = pl.BlockSpec(memory_space=pl.ANY)
+    return pl.pallas_call(
+        move_kernel,
+        out_shape=tuple(jax.ShapeDtypeStruct(a.shape, a.dtype) for a in arrays),
+        in_specs=[anywhere] * len(arrays),
+        out_specs=(anywhere,) * len(arrays),
+        scratch_shapes=[pltpu.SemaphoreType.DMA((len(arrays),))],
+        compiler_params=pltpu.CompilerParams(vmem_limit_bytes=GRANT),
+        name="move_out",
+    )(*arrays)
 
 
 def per_device(
@@ -377,12 +418,13 @@
         lax.axis_size("seq") == 2
         and data_size % 4 == 0
         and share_rows == data_size * LANES
-        and kept % 2 == 0
+        and kept % (data_size // 2) == 0
+        and kept % 4 == 0
         and upstream.shape[0] % LANES == 0
     )
     if fits:
         states = (left_gram, right_gram, left_basis, right_basis, second_moment)
-        return fused_step(acts, upstream, keep_lists, states, data_size // 4)
+        return moved(fused_step(acts, upstream, keep_lists, states, data_size // 4))
     else:
         kept_share = lax.dynamic_slice_in_dim(
             keep_lists, lax.axis_index("seq") * share_blocks, share_blocks, 0

time: 40.9 us -> 87.1 us (2.13)
  Pallas kernels: 36 us -> 86.2 us
  local copies, waits for them, and re-layouts: 3.97 us -> 0 us
    pallas_call x0 -> x1, Pallas kernels: none -> 48.8 us  [moved(): pl.pallas_call(move_kernel, out_shape=tuple((jax.ShapeDtypeStruct(a.shape...]
    unnamed x7 -> x0, local copies, waits for them, and re-layouts: 3.97 us -> none
    pallas_call x1, Pallas kernels: 36 us -> 37.5 us  [fused_step(): pl.pallas_call(functools.partial(reduce_kernel, nz, kept), out_shape=(jax...]
where the time goes in v5:
time: 87.1 us; the launch traced here: 86.9 us
  Pallas kernels  86.2 us (99%)
    pallas_call x1, Pallas kernels, moved(): pl.pallas_call(move_kernel, out_shape=tuple((jax.ShapeDtypeStruct(a.shape...  48.8 us
    pallas_call x1, Pallas kernels, fused_step(): pl.pallas_call(functools.partial(reduce_kernel, nz, kept), out_shape=(jax...  37.5 us

profile of v5, /device:TPU:0, one launch (start us, length us, event | category | flops | bytes accessed | tf_op | source)
XLA Modules:
  0.0 86.9 jit_solution(3851207387022516076)
XLA Ops:
  0.6 37.5 %fused_step.1 = (f32[1,1,16,64,64]{4,3,2,1,0:T(8,128)}, f32[1,1,16,64,64]{4,3,2,1,0:T(8,128)}, f32[1,1,16,64,64]{4,3,2,1,0:T(8,128)}) custom-call(s32[8,64]{1,0:T(8,128)} %bitcast.1, bf16[256,2048]{1,0:T(8,128)(2,1)} %acts_hbm.1, bf16[128,1024]{1,0:T(8,128)(2,1)} %up_hbm.1, f32[1,1,16,64,64]{4,3,2,1,0:T(8,128)} %left_gram.1, ...), custom_call_target="tpu_custom_call" | custom-call | flops 1073741824 | bytes 10485760 | tf_op jit(solution)/shard_map/fused_step/pallas_call | solution.py:337
  38.1 48.8 %move_out.1 = (f32[1,1,16,64,64]{4,3,2,1,0:T(8,128)}, f32[1,1,16,64,64]{4,3,2,1,0:T(8,128)}, f32[1,1,16,64,64]{4,3,2,1,0:T(8,128)}) custom-call(f32[1,1,16,64,64]{4,3,2,1,0:T(8,128)} %get-tuple-element.6.refs_0_, f32[1,1,16,64,64]{4,3,2,1,0:T(8,128)} %get-tuple-element.7.refs_1_, f32[1,1,16,64,64]{4,3,2,1,0:T(8,128)} %get-tuple-element.8.refs_2_), custom_call_target="tpu_custom_call" | custom-call | tf_op jit(solution)/shard_map/move_out/pallas_call | solution.py:399

commit v6 on v5

--- a/solution.py
+++ b/solution.py
@@ -11,6 +11,7 @@
 LANES = 128
 TOP = 32766.0
 GRANT = 65000 * 1024
+LAG = 2
 MESH = pl.DeviceIdType.MESH
 
 
@@ -69,8 +70,8 @@
 
 
 def prepare(slot, kept, low, states, ready):
-    _, _, left_basis, right_basis, moment = states
-    left_by, left_turned, right_rows, right_turned, moment_turned = ready
+    left_gram, right_gram, left_basis, right_basis, moment = states
+    left_by, left_turned, right_rows, right_turned, moment_turned, left_pair, right_pair = ready
     pair = (slot, kept + slot)
     left = jnp.concatenate([left_basis[at] for at in pair], axis=1)
     left_by[slot] = beside(diagonal(left, low))
@@ -79,11 +80,12 @@
     right_rows[slot] = rows_of(jnp.concatenate([right_basis[at] for at in pair], axis=0))
     right_turned[slot] = rows_of(jnp.concatenate([right_basis[at].T for at in pair], axis=0))
     moment_turned[slot] = jnp.concatenate([moment[at].T for at in pair], axis=1)
-
-
-def update(slots, blocks, kept, low, states, ready, outs):
-    left_gram, right_gram = states[:2]
-    left_by, left_turned, right_rows, right_turned, moment_turned = ready
+    left_pair[slot] = jnp.concatenate([left_gram[at] for at in pair], axis=1)
+    right_pair[slot] = jnp.concatenate([right_gram[at] for at in pair], axis=1)
+
+
+def update(slots, blocks, low, ready, outs):
+    left_by, left_turned, right_rows, right_turned, moment_turned, left_pair, right_pair = ready
     new_left, new_right, direction = outs
     parts = (slice(0, BLOCK), slice(BLOCK, LANES))
     partial = [stacked(rows_of(t), left_by[k]) for k, t in zip(slots, blocks)]
@@ -104,14 +106,16 @@
         inner = dot(masked[0], halves[0]) + (
             dot(masked[0], halves[1]) + dot(masked[1], halves[0])
         )
-        for part, span in enumerate(parts):
-            at = part * kept + k
-            new_left[0, 0, at] = 0.95 * left_gram[at] + 0.05 * outer[span, span]
-            new_right[0, 0, at] = 0.95 * right_gram[at] + 0.05 * inner[span]
+        down = slice(k * BLOCK, (k + 1) * BLOCK)
+        new_left[down, :] = 0.95 * left_pair[k] + 0.05 * own_halves(outer, low)
+        new_right[down, :] = 0.95 * right_pair[k] + 0.05 * jnp.concatenate(
+            [inner[span] for span in parts], axis=1
+        )
     for k, q in zip(slots, back):
         result = own_halves(stacked(right_rows[k], beside(q)), low).T
-        for part, span in enumerate(parts):
-            direction[0, 0, part * kept + k] = result[span]
+        direction[k * BLOCK : (k + 1) * BLOCK, :] = jnp.concatenate(
+            [result[span] for span in parts], axis=1
+        )
 
 
 def reduce_kernel(
@@ -119,7 +123,7 @@
     left_gram, right_gram, left_basis, right_basis, moment,
     new_left, new_right, direction,
     acts, up, upt, product, acc, states,
-    left_by, left_turned, right_rows, right_turned, moment_turned,
+    left_by, left_turned, right_rows, right_turned, moment_turned, left_pair, right_pair,
     send1, send2, send3, recv1, recv2, recv3,
     ssend1, ssend2, ssend3, srecv1, srecv2, srecv3,
     load_sems, state_sems, up_sems, sems1, sems2, sems3,
@@ -160,7 +164,9 @@
     for state_load in state_loads:
         state_load.start()
     held = tuple(states.at[i] for i in range(len(state_loads)))
-    ready = (left_by, left_turned, right_rows, right_turned, moment_turned)
+    ready = (
+        left_by, left_turned, right_rows, right_turned, moment_turned, left_pair, right_pair,
+    )
 
     barrier = pltpu.get_barrier_semaphore()
     pl.semaphore_signal(barrier, inc=1, device_id=(dp, 1 - seq), device_id_type=MESH)
@@ -287,19 +293,22 @@
             for state_load in state_loads:
                 state_load.wait()
 
-        @pl.when(step >= 1)
+        @pl.when((step >= 1) & (step <= steps))
         def _():
             for i in range(kept // steps):
                 prepare((step - 1) * (kept // steps) + i, kept, low, held, ready)
-            forward(step - 1)
-
-        @pl.when((step >= 2) & (step < steps))
-        def _():
-            spread(step - 2)
+
+        @pl.when(step >= LAG)
+        def _():
+            forward(step - LAG)
+
+        @pl.when(step >= 2 * LAG)
+        def _():
+            spread(step - 2 * LAG)
 
         return carry
 
-    lax.fori_loop(0, steps + 1, turn, 0)
+    lax.fori_loop(0, steps + LAG, turn, 0)
 
     for odd in range(2):
         slots, blocks_done = [], []
@@ -312,9 +321,7 @@
             for i in range(run):
                 slots.append(half * half_slots + odd * run + i)
                 blocks_done.append(total[i * BLOCK : (i + 1) * BLOCK])
-        update(
-            slots, blocks_done, kept, low, held, ready, (new_left, new_right, direction)
-        )
+        update(slots, blocks_done, low, ready, (new_left, new_right, direction))
 
     for half in range(2):
         for step in range(steps):
@@ -336,7 +343,7 @@
     vmem, hbm = (pl.BlockSpec(memory_space=space) for space in (pltpu.VMEM, pltpu.HBM))
     return pl.pallas_call(
         functools.partial(reduce_kernel, nz, kept),
-        out_shape=(jax.ShapeDtypeStruct(states[0].shape, jnp.float32),) * 3,
+        out_shape=(jax.ShapeDtypeStruct((kept * BLOCK, LANES), jnp.float32),) * 3,
         in_specs=[pl.BlockSpec(memory_space=pltpu.SMEM)] + [hbm] * (2 + len(states)),
         out_specs=(vmem,) * 3,
         scratch_shapes=[
@@ -350,6 +357,8 @@
             pltpu.VMEM((kept, LANES, 2 * LANES), jnp.bfloat16),
             pltpu.VMEM((kept, 2 * LANES, BLOCK), jnp.bfloat16),
             pltpu.VMEM((kept, 2 * LANES, BLOCK), jnp.bfloat16),
+            pltpu.VMEM((kept, BLOCK, LANES), jnp.float32),
+            pltpu.VMEM((kept, BLOCK, LANES), jnp.float32),
             pltpu.VMEM((kept, BLOCK, LANES), jnp.float32),
             pltpu.VMEM((2, steps, 2) + half, jnp.int16),
             pltpu.VMEM((2, steps) + half, jnp.int16),
@@ -382,28 +391,37 @@
     )(keep_lists.T, acts, upstream, *states)
 
 
-def move_kernel(*refs):
-    count = len(refs) // 2
-    sems = refs[-1]
+def unpair_kernel(kept, *refs):
+    count = (len(refs) - 2) // 2
+    staged, sems = refs[-2:]
     copies = [
-        pltpu.make_async_copy(refs[i], refs[count + i], sems.at[i]) for i in range(count)
+        pltpu.make_async_copy(staged.at[i], refs[count + i].at[0, 0], sems.at[i])
+        for i in range(count)
     ]
-    for copy in copies:
-        copy.start()
+    for i in range(count):
+        for slot in range(kept):
+            pair = refs[i][slot * BLOCK : (slot + 1) * BLOCK, :]
+            staged[i, slot] = pair[:, :BLOCK]
+            staged[i, kept + slot] = pair[:, BLOCK:]
+        copies[i].start()
     for copy in copies:
         copy.wait()
 
 
-def moved(arrays):
-    anywhere = pl.BlockSpec(memory_space=pl.ANY)
+def unpaired(arrays, shape):
+    vmem, hbm = (pl.BlockSpec(memory_space=space) for space in (pltpu.VMEM, pltpu.HBM))
+    count = len(arrays)
     return pl.pallas_call(
-        move_kernel,
-        out_shape=tuple(jax.ShapeDtypeStruct(a.shape, a.dtype) for a in arrays),
-        in_specs=[anywhere] * len(arrays),
-        out_specs=(anywhere,) * len(arrays),
-        scratch_shapes=[pltpu.SemaphoreType.DMA((len(arrays),))],
+        functools.partial(unpair_kernel, arrays[0].shape[0] // BLOCK),
+        out_shape=(jax.ShapeDtypeStruct(shape, jnp.float32),) * count,
+        in_specs=[vmem] * count,
+        out_specs=(hbm,) * count,
+        scratch_shapes=[
+            pltpu.VMEM((count,) + shape[2:], jnp.float32),
+            pltpu.SemaphoreType.DMA((count,)),
+        ],
         compiler_params=pltpu.CompilerParams(vmem_limit_bytes=GRANT),
-        name="move_out",
+        name="unpair",
     )(*arrays)
 
 
@@ -424,7 +442,8 @@
     )
     if fits:
         states = (left_gram, right_gram, left_basis, right_basis, second_moment)
-        return moved(fused_step(acts, upstream, keep_lists, states, data_size // 4))
+        pairs = fused_step(acts, upstream, keep_lists, states, data_size // 4)
+        return unpaired(pairs, left_gram.shape)
     else:
         kept_share = lax.dynamic_slice_in_dim(
             keep_lists, lax.axis_index("seq") * share_blocks, share_blocks, 0

time: 87.1 us -> 39 us (0.45)
  Pallas kernels: 86.2 us -> 38.2 us
    pallas_call x1, Pallas kernels: 48.8 us -> 2.41 us  [unpaired(): pl.pallas_call(functools.partial(unpair_kernel, arrays[0].shape[0] // BLO...]
    pallas_call x1, Pallas kernels: 37.5 us -> 35.8 us  [fused_step(): pl.pallas_call(functools.partial(reduce_kernel, nz, kept), out_shape=(jax...]
where the time goes in v6:
time: 39 us; the launch traced here: 38.9 us
  Pallas kernels  38.2 us (98%)
  between operations  0.64 us (2%)
    pallas_call x1, Pallas kernels, fused_step(): pl.pallas_call(functools.partial(reduce_kernel, nz, kept), out_shape=(jax...  35.8 us
    pallas_call x1, Pallas kernels, unpaired(): pl.pallas_call(functools.partial(unpair_kernel, arrays[0].shape[0] // BLO...  2.41 us

profile of v6, /device:TPU:0, one launch (start us, length us, event | category | flops | bytes accessed | tf_op | source)
XLA Modules:
  0.0 38.9 jit_solution(2538906119613612567)
XLA Ops:
  0.6 35.8 %fused_step.1 = (f32[512,128]{1,0:T(8,128)}, f32[512,128]{1,0:T(8,128)}, f32[512,128]{1,0:T(8,128)}) custom-call(s32[8,64]{1,0:T(8,128)} %bitcast.1, bf16[256,2048]{1,0:T(8,128)(2,1)} %acts_hbm.1, bf16[128,1024]{1,0:T(8,128)(2,1)} %up_hbm.1, f32[1,1,16,64,64]{4,3,2,1,0:T(8,128)} %left_gram.1, f32[1,1,16,64,64]{4,3,2,1,0:T(8,128)} %right_gram.1, ...), custom_call_target="tpu_custom_call" | custom-call | flops 1073741824 | bytes 10485760 | tf_op jit(solution)/shard_map/fused_step/pallas_call | solution.py:344
  36.5 2.4 %unpair.1 = (f32[1,1,16,64,64]{4,3,2,1,0:T(8,128)}, f32[1,1,16,64,64]{4,3,2,1,0:T(8,128)}, f32[1,1,16,64,64]{4,3,2,1,0:T(8,128)}) custom-call(f32[512,128]{1,0:T(8,128)} %get-tuple-element.6.refs_0_, f32[512,128]{1,0:T(8,128)} %get-tuple-element.7.refs_1_, f32[512,128]{1,0:T(8,128)} %get-tuple-element.8.refs_2_), custom_call_target="tpu_custom_call" | custom-call | tf_op jit(solution)/shard_map/unpair/pallas_call | solution.py:414

commit v7 on v6

--- a/solution.py
+++ b/solution.py
@@ -152,7 +152,7 @@
             acts_hbm.at[:, columns], acts.at[turn_z], load_sems.at[turn_z + 1]
         )
 
-    up_load = pltpu.make_async_copy(up_hbm, up, load_sems.at[0])
+    up_load = pltpu.make_async_copy(up_hbm, up.at[seq], load_sems.at[0])
     up_load.start()
     for turn_z in range(nz):
         load(turn_z).start()
@@ -172,8 +172,6 @@
     pl.semaphore_signal(barrier, inc=1, device_id=(dp, 1 - seq), device_id_type=MESH)
     for peer in (x_peer, y_peer) + tuple(z_peer(2 * turn_z) for turn_z in range(nz - 1)):
         pl.semaphore_signal(barrier, inc=1, device_id=(peer, seq), device_id_type=MESH)
-    up_load.wait()
-    upt[seq] = up[...].T
     pl.semaphore_wait(barrier, nz + 2)
 
     def remote(src, dst, sems, peer):
@@ -182,9 +180,12 @@
             device_id=peer, device_id_type=MESH,
         )
 
-    up_copy = remote(upt.at[seq], upt.at[seq], up_sems, (dp, 1 - seq))
+    up_copy = remote(up_hbm, up.at[seq], up_sems, (dp, 1 - seq))
     up_copy.start()
+    up_load.wait()
+    upt[seq] = up[seq].T
     up_copy.wait()
+    upt[1 - seq] = up[1 - seq].T
 
     half_slots = kept // 2
     run = half_slots // 2
@@ -213,44 +214,41 @@
             remote(ssend3.at[half, step], srecv3.at[half, step], sems3.at[half, step, 1], peer),
         )
 
-    def multiply(turn_z):
-        load(turn_z).wait()
-        for dy in (1, 0):
-            to_y = y if dy == 0 else oy
-            columns = pl.ds(pl.multiple_of(to_y * (2 * LANES), 2 * LANES), 2 * LANES)
-            whole = jnp.dot(
-                jnp.concatenate([upt[0], upt[1]], axis=1),
-                acts[turn_z, :, columns],
-                preferred_element_type=jnp.float32,
-            )
-            product[dy, 0] = whole[:, :LANES].reshape(-1, BLOCK, LANES)
-            product[dy, 1] = whole[:, LANES:].reshape(-1, BLOCK, LANES)
-
-    def produce(step):
-        for dy in (1, 0):
-            to_y = y if dy == 0 else oy
-            for dx in (1, 0):
-                to_x = x if dx == 0 else ox
-                row_block = seq * blocks + ((z_target(step) * 2 + to_y) * 2 + to_x) * 2
-                for half in range(2):
-                    parts = []
-                    for i in range(run):
-                        slot = half * half_slots + lax.rem(step, 2) * run + i
-                        top = keep_ref[slot, row_block]
-                        bottom = keep_ref[slot, row_block + 1]
-                        parts.append(
-                            jnp.where(low, product[dy, to_x, top], product[dy, to_x, bottom])
-                        )
-                    value = jnp.concatenate(parts, axis=0)
-                    away, place = ((dx, dy), (dy, dx))[half]
-                    if away:
-                        coded, scale = encode(value)
-                        send1[half, step, place] = coded
-                        ssend1[half, step, place] = jnp.broadcast_to(scale, (8, LANES))
-                    else:
-                        acc[half, step, place] = value
-            for copy in copies1(dy, step):
-                copy.start()
+    def multiply(turn_z, dy):
+        to_y = y if dy == 0 else oy
+        columns = pl.ds(pl.multiple_of(to_y * (2 * LANES), 2 * LANES), 2 * LANES)
+        whole = jnp.dot(
+            jnp.concatenate([upt[0], upt[1]], axis=1),
+            acts[turn_z, :, columns],
+            preferred_element_type=jnp.float32,
+        )
+        product[dy, 0] = whole[:, :LANES].reshape(-1, BLOCK, LANES)
+        product[dy, 1] = whole[:, LANES:].reshape(-1, BLOCK, LANES)
+
+    def produce(step, dy):
+        to_y = y if dy == 0 else oy
+        for dx in (1, 0):
+            to_x = x if dx == 0 else ox
+            row_block = seq * blocks + ((z_target(step) * 2 + to_y) * 2 + to_x) * 2
+            for half in range(2):
+                parts = []
+                for i in range(run):
+                    slot = half * half_slots + lax.rem(step, 2) * run + i
+                    top = keep_ref[slot, row_block]
+                    bottom = keep_ref[slot, row_block + 1]
+                    parts.append(
+                        jnp.where(low, product[dy, to_x, top], product[dy, to_x, bottom])
+                    )
+                value = jnp.concatenate(parts, axis=0)
+                away, place = ((dx, dy), (dy, dx))[half]
+                if away:
+                    coded, scale = encode(value)
+                    send1[half, step, place] = coded
+                    ssend1[half, step, place] = jnp.broadcast_to(scale, (8, LANES))
+                else:
+                    acc[half, step, place] = value
+        for copy in copies1(dy, step):
+            copy.start()
 
     def forward(step):
         for half in (1, 0):
@@ -282,11 +280,15 @@
     def turn(step, carry):
         @pl.when((step < steps) & (lax.rem(step, 2) == 0))
         def _():
-            multiply(step // 2)
-
-        @pl.when(step < steps)
-        def _():
-            produce(step)
+            load(step // 2).wait()
+            for dy in (1, 0):
+                multiply(step // 2, dy)
+                produce(step, dy)
+
+        @pl.when((step < steps) & (lax.rem(step, 2) == 1))
+        def _():
+            for dy in (1, 0):
+                produce(step, dy)
 
         @pl.when(step == 1)
         def _():
@@ -348,7 +350,7 @@
         out_specs=(vmem,) * 3,
         scratch_shapes=[
             pltpu.VMEM((nz, acts.shape[0], 4 * LANES), jnp.bfloat16),
-            pltpu.VMEM(upstream.shape, jnp.bfloat16),
+            pltpu.VMEM((2,) + upstream.shape, jnp.bfloat16),
             pltpu.VMEM((2, rows, tokens), jnp.bfloat16),
             pltpu.VMEM((2, 2, rows // BLOCK, BLOCK, LANES), jnp.float32),
             pltpu.VMEM((2, steps, 2) + half, jnp.float32),

time: 39 us -> 39.7 us (1.018)
  Pallas kernels: 38.2 us -> 38.9 us
    pallas_call x1, Pallas kernels: 35.8 us -> 36.5 us  [fused_step(): pl.pallas_call(functools.partial(reduce_kernel, nz, kept), out_shape=(jax...]
where the time goes in v7:
time: 39.7 us; the launch traced here: 39.6 us
  Pallas kernels  38.9 us (98%)
  between operations  0.64 us (2%)
    pallas_call x1, Pallas kernels, fused_step(): pl.pallas_call(functools.partial(reduce_kernel, nz, kept), out_shape=(jax...  36.5 us
    pallas_call x1, Pallas kernels, unpaired(): pl.pallas_call(functools.partial(unpair_kernel, arrays[0].shape[0] // BLO...  2.41 us

profile of v7, /device:TPU:0, one launch (start us, length us, event | category | flops | bytes accessed | tf_op | source)
XLA Modules:
  0.0 39.6 jit_solution(11653261895213354171)
XLA Ops:
  0.6 36.5 %fused_step.1 = (f32[512,128]{1,0:T(8,128)}, f32[512,128]{1,0:T(8,128)}, f32[512,128]{1,0:T(8,128)}) custom-call(s32[8,64]{1,0:T(8,128)} %bitcast.1, bf16[256,2048]{1,0:T(8,128)(2,1)} %acts_hbm.1, bf16[128,1024]{1,0:T(8,128)(2,1)} %up_hbm.1, f32[1,1,16,64,64]{4,3,2,1,0:T(8,128)} %left_gram.1, f32[1,1,16,64,64]{4,3,2,1,0:T(8,128)} %right_gram.1, ...), custom_call_target="tpu_custom_call" | custom-call | flops 1073741824 | bytes 10485760 | tf_op jit(solution)/shard_map/fused_step/pallas_call | solution.py:346
  37.2 2.4 %unpair.1 = (f32[1,1,16,64,64]{4,3,2,1,0:T(8,128)}, f32[1,1,16,64,64]{4,3,2,1,0:T(8,128)}, f32[1,1,16,64,64]{4,3,2,1,0:T(8,128)}) custom-call(f32[512,128]{1,0:T(8,128)} %get-tuple-element.6.refs_0_, f32[512,128]{1,0:T(8,128)} %get-tuple-element.7.refs_1_, f32[512,128]{1,0:T(8,128)} %get-tuple-element.8.refs_2_), custom_call_target="tpu_custom_call" | custom-call | tf_op jit(solution)/shard_map/unpair/pallas_call | solution.py:416

commit v8 on v6

--- a/solution.py
+++ b/solution.py
@@ -280,6 +280,14 @@
                 copy.start()
 
     def turn(step, carry):
+        @pl.when(step >= LAG)
+        def _():
+            forward(step - LAG)
+
+        @pl.when(step >= 2 * LAG)
+        def _():
+            spread(step - 2 * LAG)
+
         @pl.when((step < steps) & (lax.rem(step, 2) == 0))
         def _():
             multiply(step // 2)
@@ -297,14 +305,6 @@
         def _():
             for i in range(kept // steps):
                 prepare((step - 1) * (kept // steps) + i, kept, low, held, ready)
-
-        @pl.when(step >= LAG)
-        def _():
-            forward(step - LAG)
-
-        @pl.when(step >= 2 * LAG)
-        def _():
-            spread(step - 2 * LAG)
 
         return carry
 

time: 39 us -> 39.5 us (1.013)
  Pallas kernels: 38.2 us -> 38.7 us
    pallas_call x1, Pallas kernels: 35.8 us -> 36.3 us  [fused_step(): pl.pallas_call(functools.partial(reduce_kernel, nz, kept), out_shape=(jax...]
where the time goes in v8:
time: 39.5 us; the launch traced here: 39.3 us
  Pallas kernels  38.7 us (98%)
  between operations  0.64 us (2%)
    pallas_call x1, Pallas kernels, fused_step(): pl.pallas_call(functools.partial(reduce_kernel, nz, kept), out_shape=(jax...  36.3 us
    pallas_call x1, Pallas kernels, unpaired(): pl.pallas_call(functools.partial(unpair_kernel, arrays[0].shape[0] // BLO...  2.41 us

profile of v8, /device:TPU:0, one launch (start us, length us, event | category | flops | bytes accessed | tf_op | source)
XLA Modules:
  0.0 39.3 jit_solution(5415589965378471764)
XLA Ops:
  0.6 36.3 %fused_step.1 = (f32[512,128]{1,0:T(8,128)}, f32[512,128]{1,0:T(8,128)}, f32[512,128]{1,0:T(8,128)}) custom-call(s32[8,64]{1,0:T(8,128)} %bitcast.1, bf16[256,2048]{1,0:T(8,128)(2,1)} %acts_hbm.1, bf16[128,1024]{1,0:T(8,128)(2,1)} %up_hbm.1, f32[1,1,16,64,64]{4,3,2,1,0:T(8,128)} %left_gram.1, f32[1,1,16,64,64]{4,3,2,1,0:T(8,128)} %right_gram.1, ...), custom_call_target="tpu_custom_call" | custom-call | flops 1073741824 | bytes 10485760 | tf_op jit(solution)/shard_map/fused_step/pallas_call | solution.py:344
  36.9 2.4 %unpair.1 = (f32[1,1,16,64,64]{4,3,2,1,0:T(8,128)}, f32[1,1,16,64,64]{4,3,2,1,0:T(8,128)}, f32[1,1,16,64,64]{4,3,2,1,0:T(8,128)}) custom-call(f32[512,128]{1,0:T(8,128)} %get-tuple-element.6.refs_0_, f32[512,128]{1,0:T(8,128)} %get-tuple-element.7.refs_1_, f32[512,128]{1,0:T(8,128)} %get-tuple-element.8.refs_2_), custom_call_target="tpu_custom_call" | custom-call | tf_op jit(solution)/shard_map/unpair/pallas_call | solution.py:414

commit v9 on v6

--- a/solution.py
+++ b/solution.py
@@ -302,9 +302,9 @@
         def _():
             forward(step - LAG)
 
-        @pl.when(step >= 2 * LAG)
-        def _():
-            spread(step - 2 * LAG)
+        @pl.when((step > LAG) & (step <= steps))
+        def _():
+            spread(step - LAG - 1)
 
         return carry
 

time: 39 us -> 39.5 us (1.013)
  Pallas kernels: 38.2 us -> 38.6 us
    pallas_call x1, Pallas kernels: 35.8 us -> 36.2 us  [fused_step(): pl.pallas_call(functools.partial(reduce_kernel, nz, kept), out_shape=(jax...]
where the time goes in v9:
time: 39.5 us; the launch traced here: 39.3 us
  Pallas kernels  38.6 us (98%)
  between operations  0.64 us (2%)
    pallas_call x1, Pallas kernels, fused_step(): pl.pallas_call(functools.partial(reduce_kernel, nz, kept), out_shape=(jax...  36.2 us
    pallas_call x1, Pallas kernels, unpaired(): pl.pallas_call(functools.partial(unpair_kernel, arrays[0].shape[0] // BLO...  2.41 us

profile of v9, /device:TPU:0, one launch (start us, length us, event | category | flops | bytes accessed | tf_op | source)
XLA Modules:
  0.0 39.3 jit_solution(17212226037424793835)
XLA Ops:
  0.6 36.2 %fused_step.1 = (f32[512,128]{1,0:T(8,128)}, f32[512,128]{1,0:T(8,128)}, f32[512,128]{1,0:T(8,128)}) custom-call(s32[8,64]{1,0:T(8,128)} %bitcast.1, bf16[256,2048]{1,0:T(8,128)(2,1)} %acts_hbm.1, bf16[128,1024]{1,0:T(8,128)(2,1)} %up_hbm.1, f32[1,1,16,64,64]{4,3,2,1,0:T(8,128)} %left_gram.1, f32[1,1,16,64,64]{4,3,2,1,0:T(8,128)} %right_gram.1, ...), custom_call_target="tpu_custom_call" | custom-call | flops 1073741824 | bytes 10485760 | tf_op jit(solution)/shard_map/fused_step/pallas_call | solution.py:344
  36.9 2.4 %unpair.1 = (f32[1,1,16,64,64]{4,3,2,1,0:T(8,128)}, f32[1,1,16,64,64]{4,3,2,1,0:T(8,128)}, f32[1,1,16,64,64]{4,3,2,1,0:T(8,128)}) custom-call(f32[512,128]{1,0:T(8,128)} %get-tuple-element.6.refs_0_, f32[512,128]{1,0:T(8,128)} %get-tuple-element.7.refs_1_, f32[512,128]{1,0:T(8,128)} %get-tuple-element.8.refs_2_), custom_call_target="tpu_custom_call" | custom-call | tf_op jit(solution)/shard_map/unpair/pallas_call | solution.py:414
